TPU v7x, 128 devices: a whole 4x4x4 slice. The times are simulated.
128 devices in a mesh: dp: 8 (over z, core), row: 4 (over y), col: 4 (over x).
Axes of the slice: x: 4, y: 4, z: 4, core: 2. Of those that a mesh axis runs over, the one named last changes fastest.
Arguments:
- inputs: float32 [8192, 1024], P(('dp', 'row'), 'col'), may hold values from -6 to 6
- w_qkv: bfloat16 [2, 1024, 3, 1024], P(None, 'row', None, 'col'), may hold values from -0.1875 to 0.1875
- w_out: bfloat16 [2, 1024, 1024], P(None, 'row', 'col'), may hold values from -0.75 to 0.75
- w_up: bfloat16 [2, 1024, 4096], P(None, 'row', 'col'), may hold values from -0.1875 to 0.1875
- w_down: bfloat16 [2, 4096, 1024], P(None, 'row', 'col'), may hold values from -0.09375 to 0.09375
- small_params: float32 [2, 9, 1024], P(None, None, 'col'), may hold values from -0.75 to 1.875, as said below
- query_bias: float32 [2, 1024], P(None, 'col'), may hold values from -1.8 to 1.8
- up_bias: float32 [2, 4096], P(None, 'col'), may hold values from -1.8 to 1.8
- cotangent: float32 [8192, 1024], P(('dp', 'row'), 'col'), may hold values from -6 to 6
Outputs:
- output: float32 [8192, 1024], P(('dp', 'row'), 'col')
- input_grad: float32 [8192, 1024], P(('dp', 'row'), 'col')
- qkv_grad: float32 [2, 1024, 3, 1024], P(None, 'row', None, 'col')
- out_grad: float32 [2, 1024, 1024], P(None, 'row', 'col')
- up_grad: float32 [2, 1024, 4096], P(None, 'row', 'col')
- down_grad: float32 [2, 4096, 1024], P(None, 'row', 'col')
- small_grad: float32 [2, 9, 1024], P(None, None, 'col')
- query_bias_grad: float32 [2, 1024], P(None, 'col')
- up_bias_grad: float32 [2, 4096], P(None, 'col')
Inputs may be any that keep to these rules, and one draw needn't show every extreme that they name: `small_params`: norm gains and layer scales are positive.
All inputs are finite; a program needn't handle non-finite values.
Results may differ from a plain program's by a relative error of at most 0.02.
Values may be sent and summed in bfloat16 or wider, within the bound.
A program may use at most 128 MiB of HBM per device.

v0:
```python
from functools import partial

import jax
import jax.numpy as jnp
from jax import lax
from jax.sharding import PartitionSpec as P

HD = 64


EPS = 1e-06


def norm_forward(stream, gain_row, shift_row, full_width):
    row_mean = lax.psum(jnp.sum(stream, 1, keepdims=True), "col") / full_width
    centered = stream - row_mean
    variance = lax.psum(jnp.sum(centered * centered, 1, keepdims=True), "col") / full_width
    inverse = lax.rsqrt(variance + EPS)
    normed = centered * inverse
    return (normed * gain_row + shift_row, normed, inverse)


def norm_backward(upstream, normed, inverse, gain_row, full_width):
    scaled = upstream * gain_row
    first_sum, second_sum = lax.psum(
        (jnp.sum(scaled, 1, keepdims=True), jnp.sum(scaled * normed, 1, keepdims=True)), "col"
    )
    return inverse * (scaled - first_sum / full_width - normed * second_sum / full_width)


def widen(part_rows):
    return lax.all_gather(part_rows, "col", axis=1, tiled=True)


def narrow(partial_rows):
    return lax.psum_scatter(
        partial_rows.astype(jnp.bfloat16), "col", scatter_dimension=1, tiled=True
    ).astype(jnp.float32)


def left_product(activation, upstream):
    return lax.dot_general(
        activation, upstream, (((0,), (0,)), ((), ())), preferred_element_type=jnp.float32
    )


def right_product(upstream, weight_rows):
    return lax.dot_general(
        upstream, weight_rows, (((1,), (1,)), ((), ())), preferred_element_type=jnp.float32
    )


def fetch(qkv_part, out_part, up_part, down_part):
    return (
        lax.all_gather(qkv_part, "row", axis=0, tiled=True),
        lax.all_gather(out_part, "row", axis=0, tiled=True),
        lax.all_gather(up_part, "row", axis=0, tiled=True),
        lax.all_gather(down_part, "row", axis=0, tiled=True),
    )


def refetch(qkv_part, out_part, up_part, down_part):
    return (
        lax.all_gather(qkv_part, "row", axis=0, tiled=True),
        lax.all_gather(out_part, "row", axis=0, tiled=True),
        lax.all_gather(up_part, "row", axis=0, tiled=True),
        lax.all_gather(down_part, "row", axis=0, tiled=True),
    )


def reorder(partial_term, row_count, data_count):
    full_shape = partial_term.shape
    piece_rows = full_shape[0] // (row_count * data_count)
    split_rows = partial_term.reshape((row_count, data_count, piece_rows) + full_shape[1:])
    return jnp.swapaxes(split_rows, 0, 1).reshape(full_shape)


def reduce_grads(activations, upstreams, part_width):
    first_full, attended_full, second_full, activated_full = activations
    joined_grad, grad_one_low, pre_grad, grad_two_low = upstreams
    qkv_term = left_product(first_full, joined_grad).reshape(first_full.shape[1], 3, part_width)
    out_term = left_product(attended_full, grad_one_low)
    up_term = left_product(second_full, pre_grad)
    down_term = left_product(activated_full, grad_two_low)
    row_count = lax.axis_size("row")
    data_count = lax.axis_size("dp")
    pieces = (
        lax.psum_scatter(
            reorder(qkv_term, row_count, data_count).astype(jnp.bfloat16),
            ("dp", "row"),
            scatter_dimension=0,
            tiled=True,
        ).astype(jnp.float32),
        lax.psum_scatter(
            reorder(out_term, row_count, data_count).astype(jnp.bfloat16),
            ("dp", "row"),
            scatter_dimension=0,
            tiled=True,
        ).astype(jnp.float32),
        lax.psum_scatter(
            reorder(up_term, row_count, data_count).astype(jnp.bfloat16),
            ("dp", "row"),
            scatter_dimension=0,
            tiled=True,
        ).astype(jnp.float32),
        lax.psum_scatter(
            reorder(down_term, row_count, data_count).astype(jnp.bfloat16),
            ("dp", "row"),
            scatter_dimension=0,
            tiled=True,
        ).astype(jnp.float32),
    )
    return (
        lax.all_gather(pieces[0].astype(jnp.bfloat16), "dp", axis=0, tiled=True).astype(
            jnp.float32
        ),
        lax.all_gather(pieces[1].astype(jnp.bfloat16), "dp", axis=0, tiled=True).astype(
            jnp.float32
        ),
        lax.all_gather(pieces[2].astype(jnp.bfloat16), "dp", axis=0, tiled=True).astype(
            jnp.float32
        ),
        lax.all_gather(pieces[3].astype(jnp.bfloat16), "dp", axis=0, tiled=True).astype(
            jnp.float32
        ),
    )


def shards(inputs, w_qkv, w_out, w_up, w_down, small_params, query_bias, up_bias, cotangent):
    tokens, part_width = inputs.shape
    full_width = part_width * lax.axis_size("col")
    head_count = part_width // HD
    score_scale = HD ** (-0.5)
    layers = w_qkv.shape[0]
    bf16 = jnp.bfloat16
    stream = inputs
    kept_state = []
    for level in range(layers):
        layer_small = small_params[level]
        blocks = fetch(w_qkv[level], w_out[level], w_up[level], w_down[level])
        normed_in, hat_one, inv_one = norm_forward(
            stream, layer_small[0], layer_small[1], full_width
        )
        first_full = widen(normed_in.astype(bf16))
        projected = jnp.dot(
            first_full,
            blocks[0].reshape(full_width, 3 * part_width),
            preferred_element_type=jnp.float32,
        ).reshape(tokens, 3, part_width)
        queries = (projected[:, 0] + query_bias[level]).astype(bf16)
        key_rows = projected[:, 1].astype(bf16)
        value_rows = (projected[:, 2] + layer_small[2]).astype(bf16)
        all_keys, all_values = (
            lax.all_gather(key_rows, "row", axis=0, tiled=True),
            lax.all_gather(value_rows, "row", axis=0, tiled=True),
        )
        length = all_keys.shape[0]
        query_heads = queries.reshape(tokens, head_count, HD)
        key_heads = all_keys.reshape(length, head_count, HD)
        value_heads = all_values.reshape(length, head_count, HD)
        scores = (
            jnp.einsum("qhd,khd->hqk", query_heads, key_heads, preferred_element_type=jnp.float32)
            * score_scale
        )
        row_peak = jnp.max(scores, -1, keepdims=True)
        exp_scores = jnp.exp(scores - row_peak)
        row_total = jnp.sum(exp_scores, -1, keepdims=True)
        attn_probs = exp_scores / row_total
        log_total = row_peak + jnp.log(row_total)
        attended = (
            jnp.einsum(
                "hqk,khd->qhd",
                attn_probs.astype(bf16),
                value_heads,
                preferred_element_type=jnp.float32,
            )
            .reshape(tokens, part_width)
            .astype(bf16)
        )
        attended_full = widen(attended)
        branch_one = (
            jnp.dot(attended_full, blocks[1], preferred_element_type=jnp.float32) + layer_small[3]
        )
        middle = stream + layer_small[4] * branch_one
        normed_mid, hat_two, inv_two = norm_forward(
            middle, layer_small[5], layer_small[6], full_width
        )
        second_full = widen(normed_mid.astype(bf16))
        hidden_pre = (
            jnp.dot(second_full, blocks[2], preferred_element_type=jnp.float32) + up_bias[level]
        )
        activated_full = widen(jax.nn.gelu(hidden_pre, approximate=False).astype(bf16))
        branch_two = (
            jnp.dot(activated_full, blocks[3], preferred_element_type=jnp.float32) + layer_small[7]
        )
        kept_state.append(
            (
                blocks,
                hat_one,
                inv_one,
                first_full,
                query_heads,
                key_heads,
                value_heads,
                log_total,
                attended_full,
                branch_one,
                hat_two,
                inv_two,
                second_full,
                hidden_pre,
                activated_full,
                branch_two,
            )
        )
        stream = middle + layer_small[8] * branch_two
    stream_grad = cotangent
    weight_grads = [None] * layers
    small_grads = [None] * layers
    query_grads = [None] * layers
    bias_grads = [None] * layers
    for level in reversed(range(layers)):
        (
            blocks,
            hat_one,
            inv_one,
            first_full,
            query_heads,
            key_heads,
            value_heads,
            log_total,
            attended_full,
            branch_one,
            hat_two,
            inv_two,
            second_full,
            hidden_pre,
            activated_full,
            branch_two,
        ) = kept_state[level]
        blocks = refetch(w_qkv[level], w_out[level], w_up[level], w_down[level])
        layer_small = small_params[level]
        length = key_heads.shape[0]
        grad_scale_two = jnp.sum(stream_grad * branch_two, 0)
        grad_two = stream_grad * layer_small[8]
        grad_two_low = grad_two.astype(bf16)
        act_grad = narrow(right_product(grad_two_low, blocks[3]))
        gelu_pull = jax.vjp(partial(jax.nn.gelu, approximate=False), hidden_pre)[1]
        pre_grad = gelu_pull(act_grad)[0].astype(bf16)
        up_bias_grad = jnp.sum(pre_grad.astype(jnp.float32), 0)
        mid_norm_grad = narrow(right_product(pre_grad, blocks[2]))
        grad_gain_two = jnp.sum(mid_norm_grad * hat_two, 0)
        grad_shift_two = jnp.sum(mid_norm_grad, 0)
        middle_grad = stream_grad + norm_backward(
            mid_norm_grad, hat_two, inv_two, layer_small[5], full_width
        )
        grad_scale_one = jnp.sum(middle_grad * branch_one, 0)
        grad_one = middle_grad * layer_small[4]
        grad_one_low = grad_one.astype(bf16)
        attended_grad = narrow(right_product(grad_one_low, blocks[1])).astype(bf16)
        head_grads = attended_grad.reshape(tokens, head_count, HD)
        scores = (
            jnp.einsum("qhd,khd->hqk", query_heads, key_heads, preferred_element_type=jnp.float32)
            * score_scale
        )
        attn_probs = jnp.exp(scores - log_total)
        prob_grad = jnp.einsum(
            "qhd,khd->hqk", head_grads, value_heads, preferred_element_type=jnp.float32
        )
        inner_sum = jnp.sum(attn_probs * prob_grad, -1, keepdims=True)
        score_grad = (attn_probs * (prob_grad - inner_sum)).astype(bf16)
        query_grad = (
            jnp.einsum("hqk,khd->qhd", score_grad, key_heads, preferred_element_type=jnp.float32)
            * score_scale
        )
        key_term = (
            jnp.einsum("hqk,qhd->khd", score_grad, query_heads, preferred_element_type=jnp.float32)
            * score_scale
        )
        value_term = jnp.einsum(
            "hqk,qhd->khd", attn_probs.astype(bf16), head_grads, preferred_element_type=jnp.float32
        )
        key_grad, value_grad = (
            lax.psum_scatter(
                key_term.reshape(length, part_width).astype(jnp.bfloat16),
                "row",
                scatter_dimension=0,
                tiled=True,
            ).astype(jnp.float32),
            lax.psum_scatter(
                value_term.reshape(length, part_width).astype(jnp.bfloat16),
                "row",
                scatter_dimension=0,
                tiled=True,
            ).astype(jnp.float32),
        )
        joined_grad = jnp.stack([query_grad.reshape(tokens, part_width), key_grad, value_grad], 1)
        joined_grad = joined_grad.astype(bf16).reshape(tokens, 3 * part_width)
        grad_query_bias = jnp.sum(joined_grad[:, :part_width].astype(jnp.float32), 0)
        grad_value_bias = jnp.sum(joined_grad[:, 2 * part_width :].astype(jnp.float32), 0)
        in_norm_grad = narrow(
            right_product(joined_grad, blocks[0].reshape(full_width, 3 * part_width))
        )
        grad_gain_one = jnp.sum(in_norm_grad * hat_one, 0)
        grad_shift_one = jnp.sum(in_norm_grad, 0)
        stream_grad = middle_grad + norm_backward(
            in_norm_grad, hat_one, inv_one, layer_small[0], full_width
        )
        weight_grads[level] = reduce_grads(
            (first_full, attended_full, second_full, activated_full),
            (joined_grad, grad_one_low, pre_grad, grad_two_low),
            part_width,
        )
        small_grads[level] = jnp.stack(
            [
                grad_gain_one,
                grad_shift_one,
                grad_value_bias,
                jnp.sum(grad_one, 0),
                grad_scale_one,
                grad_gain_two,
                grad_shift_two,
                jnp.sum(grad_two, 0),
                grad_scale_two,
            ]
        )
        query_grads[level] = grad_query_bias
        bias_grads[level] = up_bias_grad
    small_total, query_total, bias_total = lax.psum(
        (jnp.stack(small_grads), jnp.stack(query_grads), jnp.stack(bias_grads)), ("dp", "row")
    )
    return (
        stream,
        stream_grad,
        jnp.stack([entry[0] for entry in weight_grads]),
        jnp.stack([entry[1] for entry in weight_grads]),
        jnp.stack([entry[2] for entry in weight_grads]),
        jnp.stack([entry[3] for entry in weight_grads]),
        small_total,
        query_total,
        bias_total,
    )


def solution(mesh):
    placed = (
        P(("dp", "row"), "col"),
        P(None, "row", None, "col"),
        P(None, "row", "col"),
        P(None, "row", "col"),
        P(None, "row", "col"),
        P(None, None, "col"),
        P(None, "col"),
        P(None, "col"),
        P(("dp", "row"), "col"),
    )
    return jax.shard_map(
        shards,
        mesh=mesh,
        in_specs=placed,
        out_specs=(
            P(("dp", "row"), "col"),
            P(("dp", "row"), "col"),
            P(None, "row", None, "col"),
            P(None, "row", "col"),
            P(None, "row", "col"),
            P(None, "row", "col"),
            P(None, None, "col"),
            P(None, "col"),
            P(None, "col"),
        ),
        check_vma=False,
    )
```

profile of v0, /device:TPU:1, one launch (start us, length us, event | category | flops | bytes accessed | tf_op | source)
XLA Modules:
  0.0 1393.4 jit_solution(5386781577144225373)
XLA Ops:
  13.2 9.3 psum.133
  31.2 10.7 all_gather.92
  41.9 10.4 all-gather.2
  55.2 13.9 %all-gather.1 = bf16[1024,1,256]{0,2,1:T(8,128)(2,1)S(1)} all-gather(bf16[256,1,256]{0,2,1:T(8,128)(2,1)S(1)} %slice.247), channel_id=3, replica_groups=mesh['dp'=8,'row'=4,'col'=4] {'row'}, dimensions={0}, use_global_device_ids=true | all-gather | bytes 655360 | tf_op jit(solution)/shard_map/all_gather | solution.py:154
  70.9 12.3 all_gather.94
  84.4 9.9 all_gather.96
  95.4 8.2 psum.135
  110.9 9.9 all_gather.98
  128.1 13.5 all-gather.7
  147.1 29.9 %all-gather.27.cloned.1.call-done = bf16[1,4096,256]{2,1,0:T(8,128)(2,1)} async-done(((bf16[1,1024,256]{2,1,0:T(8,128)(2,1)}), bf16[1,4096,256]{2,1,0:T(8,128)(2,1)}) %all-gather.27.cloned.1.call-update) | async-done | bytes 2097168 | tf_op jit(solution)/shard_map/all_gather | solution.py:58
  177.0 32.4 %all-gather.19.cloned.1.call-done = bf16[256,4096]{1,0:T(8,128)(2,1)} async-done(((bf16[256,1024]{1,0:T(8,128)(2,1)}), bf16[256,4096]{1,0:T(8,128)(2,1)}) %all-gather.19.cloned.1.call-update) | async-done | bytes 2097168 | tf_op jit(solution)/shard_map/all_gather | solution.py:32
  213.0 6.5 psum.137
  219.7 7.3 psum.138
  227.2 11.1 all_gather.102
  239.0 10.2 all-gather.6
  249.3 11.1 all_gather.104
  264.5 12.7 all_gather.106
  278.2 8.0 psum.139
  292.6 10.6 all_gather.108
  303.2 7.0 convert_reduce_fusion
  315.4 33.1 %reduce-scatter.23.cloned.1.call-done = bf16[256,256]{1,0:T(8,128)(2,1)} async-done(((bf16[256,1024]{1,0:T(8,128)(2,1)}), bf16[256,256]{1,0:T(8,128)(2,1)}) %reduce-scatter.23.cloned.1.call-update) | async-done | bytes 131088 | tf_op jit(solution)/shard_map/reduce_scatter | solution.py:36
  350.2 6.6 all-reduce.4
  356.8 25.6 %all-gather.21.cloned.1.call-done = bf16[256,4096]{1,0:T(8,128)(2,1)} async-done(((bf16[256,1024]{1,0:T(8,128)(2,1)}), bf16[256,4096]{1,0:T(8,128)(2,1)}) %all-gather.21.cloned.1.call-update) | async-done | bytes 2097168 | tf_op jit(solution)/shard_map/all_gather | solution.py:32
  387.9 19.9 %reduce-scatter.25.cloned.1.call-done = bf16[256,256]{1,0:T(8,128)(2,1)} async-done(((bf16[256,1024]{1,0:T(8,128)(2,1)}), bf16[256,256]{1,0:T(8,128)(2,1)}) %reduce-scatter.25.cloned.1.call-update) | async-done | bytes 131088 | tf_op jit(solution)/shard_map/reduce_scatter | solution.py:36
  424.9 9.3 reduce-scatter.29.cloned.1.call-done
  434.2 23.7 %reduce-scatter.27.cloned.1.call-done = bf16[256,256]{1,0:T(8,128)(2,1)} async-done(((bf16[1024,256]{1,0:T(8,128)(2,1)}), bf16[256,256]{1,0:T(8,128)(2,1)}) %reduce-scatter.27.cloned.1.call-update) | async-done | bytes 131088 | tf_op jit(solution)/shard_map/reduce_scatter | solution.py:284
  461.1 21.2 %reduce-scatter.31.cloned.1.call-done = bf16[256,256]{1,0:T(8,128)(2,1)} async-done(((bf16[256,1024]{1,0:T(8,128)(2,1)}), bf16[256,256]{1,0:T(8,128)(2,1)}) %reduce-scatter.31.cloned.1.call-update) | async-done | bytes 131088 | tf_op jit(solution)/shard_map/reduce_scatter | solution.py:36
  484.1 7.2 all-reduce.3
  496.7 32.9 %reduce-scatter.33.cloned.1.call-done = bf16[256,1024]{1,0:T(8,128)(2,1)} async-done(((bf16[256,4096]{1,0:T(8,128)(2,1)}), bf16[256,1024]{1,0:T(8,128)(2,1)}) %reduce-scatter.33.cloned.1.call-update) | async-done | bytes 524304 | tf_op jit(solution)/shard_map/reduce_scatter | solution.py:36
  534.0 19.5 %reduce-scatter.35.cloned.1.call-done = bf16[256,256]{1,0:T(8,128)(2,1)} async-done(((bf16[256,1024]{1,0:T(8,128)(2,1)}), bf16[256,256]{1,0:T(8,128)(2,1)}) %reduce-scatter.35.cloned.1.call-update) | async-done | bytes 131088 | tf_op jit(solution)/shard_map/reduce_scatter | solution.py:36
  564.7 23.0 %reduce-scatter.37.cloned.1.call-done = bf16[256,256]{1,0:T(8,128)(2,1)} async-done(((bf16[256,1024]{1,0:T(8,128)(2,1)}), bf16[256,256]{1,0:T(8,128)(2,1)}) %reduce-scatter.37.cloned.1.call-update) | async-done | bytes 131088 | tf_op jit(solution)/shard_map/reduce_scatter | solution.py:36
  641.1 79.4 %reduce-scatter.55.cloned.1.call-done = bf16[32,1024]{1,0:T(8,128)(2,1)} async-done(((bf16[1024,1024]{1,0:T(8,128)(2,1)}), bf16[32,1024]{1,0:T(8,128)(2,1)}) %reduce-scatter.55.cloned.1.call-update) | async-done | bytes 65552 | tf_op jit(solution)/shard_map/reduce_scatter | solution.py:100
  720.5 15.4 %all_gather.117 = bf16[256,1024]{1,0:T(8,128)(2,1)S(1)} all-gather(bf16[32,1024]{1,0:T(8,128)(2,1)} %reduce-scatter.55.cloned.1.call-done), channel_id=1, replica_groups=mesh['dp'=8,'row'=4,'col'=4] {'dp'}, dimensions={0}, use_global_device_ids=true | all-gather | bytes 589824 | tf_op jit(solution)/shard_map/all_gather | solution.py:120
  735.9 64.2 %reduce-scatter.51.cloned.1.call-done = bf16[32,256]{1,0:T(8,128)(2,1)} async-done(((bf16[1024,256]{1,0:T(8,128)(2,1)}), bf16[32,256]{1,0:T(8,128)(2,1)}) %reduce-scatter.51.cloned.1.call-update) | async-done | bytes 16400 | tf_op jit(solution)/shard_map/reduce_scatter | solution.py:94
  800.1 15.3 %all_gather.115 = bf16[256,256]{1,0:T(8,128)(2,1)S(1)} all-gather(bf16[32,256]{1,0:T(8,128)(2,1)} %reduce-scatter.51.cloned.1.call-done), channel_id=1, replica_groups=mesh['dp'=8,'row'=4,'col'=4] {'dp'}, dimensions={0}, use_global_device_ids=true | all-gather | bytes 147456 | tf_op jit(solution)/shard_map/all_gather | solution.py:117
  817.9 64.3 %reduce-scatter.59.cloned.1.call-done = bf16[128,256]{1,0:T(8,128)(2,1)} async-done(((bf16[4096,256]{1,0:T(8,128)(2,1)}), bf16[128,256]{1,0:T(8,128)(2,1)}) %reduce-scatter.59.cloned.1.call-update) | async-done | bytes 65552 | tf_op jit(solution)/shard_map/reduce_scatter | solution.py:106
  882.2 15.4 %all_gather.119 = bf16[1024,256]{1,0:T(8,128)(2,1)S(1)} all-gather(bf16[128,256]{1,0:T(8,128)(2,1)} %reduce-scatter.59.cloned.1.call-done), channel_id=1, replica_groups=mesh['dp'=8,'row'=4,'col'=4] {'dp'}, dimensions={0}, use_global_device_ids=true | all-gather | bytes 589824 | tf_op jit(solution)/shard_map/all_gather | solution.py:123
  897.6 66.3 %reduce-scatter.47.cloned.1.call-done = bf16[32,3,256]{2,0,1:T(8,128)(2,1)} async-done(((bf16[1024,3,256]{2,0,1:T(8,128)(2,1)}), bf16[32,3,256]{2,0,1:T(8,128)(2,1)}) %reduce-scatter.47.cloned.1.call-update) | async-done | bytes 49168 | tf_op jit(solution)/shard_map/reduce_scatter | solution.py:88
  963.9 15.3 %all_gather.113 = bf16[256,3,256]{2,0,1:T(8,128)(2,1)S(1)} all-gather(bf16[32,3,256]{2,0,1:T(8,128)(2,1)} %reduce-scatter.47.cloned.1.call-done), channel_id=1, replica_groups=mesh['dp'=8,'row'=4,'col'=4] {'dp'}, dimensions={0}, use_global_device_ids=true | all-gather | bytes 442368 | tf_op jit(solution)/shard_map/all_gather | solution.py:114
  979.2 66.4 %reduce-scatter.57.cloned.1.call-done = bf16[128,256]{1,0:T(8,128)(2,1)} async-done(((bf16[4096,256]{1,0:T(8,128)(2,1)}), bf16[128,256]{1,0:T(8,128)(2,1)}) %reduce-scatter.57.cloned.1.call-update) | async-done | bytes 65552 | tf_op jit(solution)/shard_map/reduce_scatter | solution.py:106
  1045.6 15.4 %all_gather.118 = bf16[1024,256]{1,0:T(8,128)(2,1)S(1)} all-gather(bf16[128,256]{1,0:T(8,128)(2,1)} %reduce-scatter.57.cloned.1.call-done), channel_id=1, replica_groups=mesh['dp'=8,'row'=4,'col'=4] {'dp'}, dimensions={0}, use_global_device_ids=true | all-gather | bytes 589824 | tf_op jit(solution)/shard_map/all_gather | solution.py:123
  1062.5 62.7 %reduce-scatter.49.cloned.1.call-done = bf16[32,256]{1,0:T(8,128)(2,1)} async-done(((bf16[1024,256]{1,0:T(8,128)(2,1)}), bf16[32,256]{1,0:T(8,128)(2,1)}) %reduce-scatter.49.cloned.1.call-update) | async-done | bytes 16400 | tf_op jit(solution)/shard_map/reduce_scatter | solution.py:94
  1125.2 15.3 %all_gather.114 = bf16[256,256]{1,0:T(8,128)(2,1)S(1)} all-gather(bf16[32,256]{1,0:T(8,128)(2,1)} %reduce-scatter.49.cloned.1.call-done), channel_id=1, replica_groups=mesh['dp'=8,'row'=4,'col'=4] {'dp'}, dimensions={0}, use_global_device_ids=true | all-gather | bytes 147456 | tf_op jit(solution)/shard_map/all_gather | solution.py:117
  1141.4 66.3 %reduce-scatter.53.cloned.1.call-done = bf16[32,1024]{1,0:T(8,128)(2,1)} async-done(((bf16[1024,1024]{1,0:T(8,128)(2,1)}), bf16[32,1024]{1,0:T(8,128)(2,1)}) %reduce-scatter.53.cloned.1.call-update) | async-done | bytes 65552 | tf_op jit(solution)/shard_map/reduce_scatter | solution.py:100
  1207.7 15.4 %all_gather.116 = bf16[256,1024]{1,0:T(8,128)(2,1)S(1)} all-gather(bf16[32,1024]{1,0:T(8,128)(2,1)} %reduce-scatter.53.cloned.1.call-done), channel_id=1, replica_groups=mesh['dp'=8,'row'=4,'col'=4] {'dp'}, dimensions={0}, use_global_device_ids=true | all-gather | bytes 589824 | tf_op jit(solution)/shard_map/all_gather | solution.py:120
  1231.8 124.1 %all-reduce = (f32[2,9,256]{2,1,0:T(8,128)S(1)}, f32[2,256]{1,0:T(2,128)}, f32[2,1024]{1,0:T(2,128)}) all-reduce(f32[2,9,256]{2,1,0:T(8,128)S(1)} %pad_maximum_fusion, f32[2,256]{1,0:T(2,128)S(1)} %pad_maximum_fusion.2, f32[2,1024]{1,0:T(2,128)S(1)} %pad_maximum_fusion.1), channel_id=1, replica_groups=mesh['dp'=8,'row'=4,'col'=4] {'dp','row'}, use_global_device_ids=true, to_apply=%region_76.0 | all-reduce | flops 7168 | bytes 57344 | tf_op jit(solution)/shard_map/psum | solution.py:329
  1356.5 6.5 all-reduce.1
  1364.9 20.0 %all_gather.112 = bf16[256,3,256]{2,0,1:T(8,128)(2,1)S(1)} all-gather(bf16[32,3,256]{2,0,1:T(8,128)(2,1)} %reduce-scatter.45.cloned.1.call-done), channel_id=1, replica_groups=mesh['dp'=8,'row'=4,'col'=4] {'dp'}, dimensions={0}, use_global_device_ids=true | all-gather | bytes 442368 | tf_op jit(solution)/shard_map/all_gather | solution.py:114
  (396 shorter events, 182.6 us)
Async XLA Ops:
  7.2 45.2 %all-gather.23.cloned.1.call-start = ((), (), s32[]{:S(2)}) async-start(), calls=%async_computation.42 | async-start | bytes 1966080 | tf_op jit(solution)/shard_map/all_gather | solution.py:55
  9.4 111.5 %all-gather.25.cloned.1.call-start = ((), (), s32[]{:S(2)}) async-start(), calls=%async_computation.43 | async-start | bytes 2621440 | tf_op jit(solution)/shard_map/all_gather | solution.py:57
  10.5 131.1 %all-gather.29.cloned.1.call-start = ((), (), s32[]{:S(2)}) async-start(), calls=%async_computation.45 | async-start | bytes 1966080 | tf_op jit(solution)/shard_map/all_gather | solution.py:55
  11.3 132.1 %all-gather.33.cloned.1.call-start = ((), (), s32[]{:S(2)}) async-start(), calls=%async_computation.47 | async-start | bytes 2621440 | tf_op jit(solution)/shard_map/all_gather | solution.py:58
  12.4 164.6 %all-gather.27.cloned.1.call-start = ((), (), s32[]{:S(2)}) async-start(), calls=%async_computation.44 | async-start | bytes 2621440 | tf_op jit(solution)/shard_map/all_gather | solution.py:58
  13.0 196.3 %all-gather.19.cloned.1.call-start = ((), (), s32[]{:S(2)}) async-start(), calls=%async_computation.20 | async-start | bytes 2621440 | tf_op jit(solution)/shard_map/all_gather | solution.py:32
  126.6 176.6 %all-gather.31.cloned.1.call-start = ((), (), s32[]{:S(2)}) async-start(), calls=%async_computation.46 | async-start | bytes 2621440 | tf_op jit(solution)/shard_map/all_gather | solution.py:57
  127.4 175.9 %reduce-scatter.21.cloned.1.call-start = ((), (), s32[]{:S(2)}) async-start(), calls=%async_computation.22 | async-start | bytes 2621440 | tf_op jit(solution)/shard_map/reduce_scatter | solution.py:36
  147.1 201.4 %reduce-scatter.23.cloned.1.call-start = ((), (), s32[]{:S(2)}) async-start(), calls=%async_computation.23 | async-start | bytes 655360 | tf_op jit(solution)/shard_map/reduce_scatter | solution.py:36
  312.7 69.7 %all-gather.21.cloned.1.call-start = ((), (), s32[]{:S(2)}) async-start(), calls=%async_computation.21 | async-start | bytes 2621440 | tf_op jit(solution)/shard_map/all_gather | solution.py:32
  315.3 92.4 %reduce-scatter.25.cloned.1.call-start = ((), (), s32[]{:S(2)}) async-start(), calls=%async_computation.24 | async-start | bytes 655360 | tf_op jit(solution)/shard_map/reduce_scatter | solution.py:36
  387.8 46.4 %reduce-scatter.29.cloned.1.call-start = ((), (), s32[]{:S(2)}) async-start(), calls=%async_computation.26 | async-start | bytes 655360 | tf_op jit(solution)/shard_map/reduce_scatter | solution.py:290
  412.9 45.1 %reduce-scatter.27.cloned.1.call-start = ((), (), s32[]{:S(2)}) async-start(), calls=%async_computation.25 | async-start | bytes 655360 | tf_op jit(solution)/shard_map/reduce_scatter | solution.py:284
  421.4 60.9 %reduce-scatter.31.cloned.1.call-start = ((), (), s32[]{:S(2)}) async-start(), calls=%async_computation.27 | async-start | bytes 655360 | tf_op jit(solution)/shard_map/reduce_scatter | solution.py:36
  461.1 68.6 %reduce-scatter.33.cloned.1.call-start = ((), (), s32[]{:S(2)}) async-start(), calls=%async_computation.28 | async-start | bytes 2621440 | tf_op jit(solution)/shard_map/reduce_scatter | solution.py:36
  496.6 56.9 %reduce-scatter.35.cloned.1.call-start = ((), (), s32[]{:S(2)}) async-start(), calls=%async_computation.29 | async-start | bytes 655360 | tf_op jit(solution)/shard_map/reduce_scatter | solution.py:36
  533.9 53.8 %reduce-scatter.37.cloned.1.call-start = ((), (), s32[]{:S(2)}) async-start(), calls=%async_computation.30 | async-start | bytes 655360 | tf_op jit(solution)/shard_map/reduce_scatter | solution.py:36
  564.6 68.6 %reduce-scatter.41.cloned.1.call-start = ((), (), s32[]{:S(2)}) async-start(), calls=%async_computation.32 | async-start | bytes 655360 | tf_op jit(solution)/shard_map/reduce_scatter | solution.py:290
  592.9 44.9 %reduce-scatter.39.cloned.1.call-start = ((), (), s32[]{:S(2)}) async-start(), calls=%async_computation.31 | async-start | bytes 655360 | tf_op jit(solution)/shard_map/reduce_scatter | solution.py:284
  601.2 119.3 %reduce-scatter.55.cloned.1.call-start = ((), (), s32[]{:S(2)}) async-start(), calls=%async_computation.39 | async-start | bytes 2162688 | tf_op jit(solution)/shard_map/reduce_scatter | solution.py:100
  604.8 195.3 %reduce-scatter.51.cloned.1.call-start = ((), (), s32[]{:S(2)}) async-start(), calls=%async_computation.37 | async-start | bytes 540672 | tf_op jit(solution)/shard_map/reduce_scatter | solution.py:94
  607.9 274.3 %reduce-scatter.59.cloned.1.call-start = ((), (), s32[]{:S(2)}) async-start(), calls=%async_computation.41 | async-start | bytes 2162688 | tf_op jit(solution)/shard_map/reduce_scatter | solution.py:106
  612.1 351.8 %reduce-scatter.47.cloned.1.call-start = ((), (), s32[]{:S(2)}) async-start(), calls=%async_computation.35 | async-start | bytes 1622016 | tf_op jit(solution)/shard_map/reduce_scatter | solution.py:88
  620.8 424.8 %reduce-scatter.57.cloned.1.call-start = ((), (), s32[]{:S(2)}) async-start(), calls=%async_computation.40 | async-start | bytes 2162688 | tf_op jit(solution)/shard_map/reduce_scatter | solution.py:106
  624.6 500.5 %reduce-scatter.49.cloned.1.call-start = ((), (), s32[]{:S(2)}) async-start(), calls=%async_computation.36 | async-start | bytes 540672 | tf_op jit(solution)/shard_map/reduce_scatter | solution.py:94
  627.8 579.9 %reduce-scatter.53.cloned.1.call-start = ((), (), s32[]{:S(2)}) async-start(), calls=%async_computation.38 | async-start | bytes 2162688 | tf_op jit(solution)/shard_map/reduce_scatter | solution.py:100
  631.3 599.3 %reduce-scatter.43.cloned.1.call-start = ((), (), s32[]{:S(2)}) async-start(), calls=%async_computation.33 | async-start | bytes 655360 | tf_op jit(solution)/shard_map/reduce_scatter | solution.py:36
  637.8 177.7 %copy-start.24 = (bf16[256,3,256]{0,2,1:T(8,128)(2,1)S(1)}, bf16[256,3,256]{0,2,1:T(8,128)(2,1)}, u32[]{:S(2)}) copy-start(bf16[256,3,256]{0,2,1:T(8,128)(2,1)} %copy-done.23) | copy-start | bytes 1179652
  637.8 177.8 %copy-start.74 = (f32[256]{0:T(256)S(1)}, f32[256]{0:T(256)}, u32[]{:S(2)}) copy-start(f32[256]{0:T(256)} %get-tuple-element.22) | copy-start | bytes 3076
  637.8 177.8 %copy-start.75 = (f32[256]{0:T(256)S(1)}, f32[256]{0:T(256)}, u32[]{:S(2)}) copy-start(f32[256]{0:T(256)} %get-tuple-element.44) | copy-start | bytes 3076
  637.8 177.8 %copy-start.82 = (f32[256]{0:T(256)S(1)}, f32[256]{0:T(256)}, u32[]{:S(2)}) copy-start(f32[256]{0:T(256)} %get-tuple-element.24) | copy-start | bytes 3076
  637.8 177.8 %copy-start.83 = (f32[256]{0:T(256)S(1)}, f32[256]{0:T(256)}, u32[]{:S(2)}) copy-start(f32[256]{0:T(256)} %get-tuple-element.45) | copy-start | bytes 3076
  637.8 177.8 %copy-start.95 = (f32[256]{0:T(256)S(1)}, f32[256]{0:T(256)}, u32[]{:S(2)}) copy-start(f32[256]{0:T(256)} %get-tuple-element.34) | copy-start | bytes 3076
  637.8 177.8 %copy-start.96 = (f32[256]{0:T(256)S(1)}, f32[256]{0:T(256)}, u32[]{:S(2)}) copy-start(f32[256]{0:T(256)} %get-tuple-element.35) | copy-start | bytes 3076
  637.8 177.8 %copy-start.97 = (f32[256]{0:T(256)S(1)}, f32[256]{0:T(256)}, u32[]{:S(2)}) copy-start(f32[256]{0:T(256)} %get-tuple-element.82) | copy-start | bytes 3076
  637.8 177.8 %copy-start.98 = (f32[256]{0:T(256)S(1)}, f32[256]{0:T(256)}, u32[]{:S(2)}) copy-start(f32[256]{0:T(256)} %get-tuple-element.83) | copy-start | bytes 3076
  640.8 174.9 %copy-start.43 = (bf16[256,256]{1,0:T(8,128)(2,1)S(1)}, bf16[256,256]{1,0:T(8,128)(2,1)}, u32[]{:S(2)}) copy-start(bf16[256,256]{1,0:T(8,128)(2,1)} %reduce-scatter.41.cloned.1.call-done) | copy-start | bytes 393220
  640.8 174.9 %copy-start.44 = (bf16[256,256]{1,0:T(8,128)(2,1)S(1)}, bf16[256,256]{1,0:T(8,128)(2,1)}, u32[]{:S(2)}) copy-start(bf16[256,256]{1,0:T(8,128)(2,1)} %reduce-scatter.39.cloned.1.call-done) | copy-start | bytes 393220
  640.9 724.0 %reduce-scatter.45.cloned.1.call-start = ((), (), s32[]{:S(2)}) async-start(), calls=%async_computation.34 | async-start | bytes 1622016 | tf_op jit(solution)/shard_map/reduce_scatter | solution.py:88
  897.6 164.8 %copy-start.59 = (f32[1024]{0:T(1024)S(1)}, f32[1024]{0:T(1024)}, u32[]{:S(2)}) copy-start(f32[1024]{0:T(1024)} %get-tuple-element.59) | copy-start | bytes 12292
  897.6 164.8 %copy-start.91 = (f32[1024]{0:T(1024)S(1)}, f32[1024]{0:T(1024)}, u32[]{:S(2)}) copy-start(f32[1024]{0:T(1024)} %get-tuple-element.61) | copy-start | bytes 12292
  1141.4 90.3 %copy-start.76 = (f32[256]{0:T(256)S(1)}, f32[256]{0:T(256)}, u32[]{:S(2)}) copy-start(f32[256]{0:T(256)} %get-tuple-element.30) | copy-start | bytes 3076
  1141.4 90.3 %copy-start.77 = (f32[256]{0:T(256)S(1)}, f32[256]{0:T(256)}, u32[]{:S(2)}) copy-start(f32[256]{0:T(256)} %get-tuple-element.31) | copy-start | bytes 3076
  1141.4 90.3 %copy-start.78 = (f32[256]{0:T(256)S(1)}, f32[256]{0:T(256)}, u32[]{:S(2)}) copy-start(f32[256]{0:T(256)} %get-tuple-element.18) | copy-start | bytes 3076
  1141.4 90.3 %copy-start.79 = (f32[256]{0:T(256)S(1)}, f32[256]{0:T(256)}, u32[]{:S(2)}) copy-start(f32[256]{0:T(256)} %get-tuple-element.42) | copy-start | bytes 3076
  1141.4 90.3 %copy-start.80 = (f32[256]{0:T(256)S(1)}, f32[256]{0:T(256)}, u32[]{:S(2)}) copy-start(f32[256]{0:T(256)} %get-tuple-element.32) | copy-start | bytes 3076
  1141.4 90.3 %copy-start.81 = (f32[256]{0:T(256)S(1)}, f32[256]{0:T(256)}, u32[]{:S(2)}) copy-start(f32[256]{0:T(256)} %get-tuple-element.33) | copy-start | bytes 3076
  1223.1 140.0 %copy-start.22 = (f32[256,256]{1,0:T(8,128)S(1)}, f32[256,256]{1,0:T(8,128)}, u32[]{:S(2)}) copy-start(f32[256,256]{1,0:T(8,128)} %copy-done.21) | copy-start | bytes 786436
  (82 other events, 1815.8 us)
Sparse Core Ops, SparseCore 0:
  10.3 29.7 all-gather.22
  42.3 36.4 all-gather.24
  80.5 27.6 all-gather.28
  110.2 32.8 all-gather.32
  144.7 32.2 all-gather.26
  178.5 30.7 all-gather.18
  211.6 30.9 all-gather.30
  245.6 31.4 reduce-scatter.20
  312.8 35.6 reduce-scatter.22
  350.1 32.2 all-gather.20
  388.0 19.7 reduce-scatter.24
  413.0 21.1 reduce-scatter.28
  436.7 21.1 reduce-scatter.26
  461.2 21.0 reduce-scatter.30
  496.7 32.8 reduce-scatter.32
  534.0 19.4 reduce-scatter.34
  564.7 22.8 reduce-scatter.36
  593.0 21.1 reduce-scatter.40
  616.6 21.1 reduce-scatter.38
  641.8 78.7 reduce-scatter.54
  724.0 76.0 reduce-scatter.50
  803.6 78.5 reduce-scatter.58
  886.3 77.5 reduce-scatter.46
  967.3 78.2 reduce-scatter.56
  1049.0 76.1 reduce-scatter.48
  1129.2 78.4 reduce-scatter.52
  1209.9 20.5 reduce-scatter.42
  1234.1 78.1 reduce-scatter.44
where the time goes:
time: 1400 us; the launch traced here: 1390 us
  waiting for transfers between devices  753 us (54%)
  blocking collectives  473 us (34%)
  matrix products  78.1 us (6%)
  local copies, waits for them, and re-layouts  41.5 us (3%)
  other arithmetic  30.4 us (2%)
  between operations  16.1 us (1%)
    reduce_scatter x8, waiting for transfers between devices, narrow(): lax.psum_scatter(partial_rows.astype(jnp.bfloat16), 'col', scatter_dimens...  155 us
    reduce_scatter x2, waiting for transfers between devices, reduce_grads(): lax.psum_scatter(reorder(up_term, row_count, data_count).astype(jnp.bfloa...  146 us
    reduce_scatter x2, waiting for transfers between devices, reduce_grads(): lax.psum_scatter(reorder(down_term, row_count, data_count).astype(jnp.bfl...  131 us
    reduce_scatter x2, waiting for transfers between devices, reduce_grads(): lax.psum_scatter(reorder(out_term, row_count, data_count).astype(jnp.bflo...  127 us
    psum x1, blocking collectives, shards(): lax.psum((jnp.stack(small_grads), jnp.stack(query_grads), jnp.stack(bias_...  124 us
    reduce_scatter x2, waiting for transfers between devices, reduce_grads(): lax.psum_scatter(reorder(qkv_term, row_count, data_count).astype(jnp.bflo...  66.3 us
    all_gather x6, blocking collectives, widen(): return lax.all_gather(part_rows, 'col', axis=1, tiled=True)  64.9 us
    all_gather x2, waiting for transfers between devices, widen(): return lax.all_gather(part_rows, 'col', axis=1, tiled=True)  58 us
  transfers between devices with their start and end apart: 28, of which 20 were waited for; matrix products, arithmetic and copies ran while one was open for 7% of the time, Pallas kernels for 0%

commit v1 on v0

v1 whole, which is shorter than its diff:
```python
from functools import partial

import jax
import jax.numpy as jnp
from jax import lax
from jax.experimental import pallas as pl
from jax.experimental.pallas import tpu as pltpu
from jax.sharding import PartitionSpec as P

HD = 64
EPS = 1e-06
LANES = 128
BF = jnp.bfloat16
F32 = jnp.float32
MESH = pl.DeviceIdType.MESH


def mm(left, right):
    return jnp.dot(left, right, preferred_element_type=F32)


def mm_nt(left, right):
    return lax.dot_general(left, right, (((1,), (1,)), ((), ())), preferred_element_type=F32)


def mm_tn(left, right):
    return lax.dot_general(left, right, (((0,), (0,)), ((), ())), preferred_element_type=F32)


class Links:
    def __init__(self, sizes, send, recv, local):
        self.sizes = sizes
        self.send, self.recv, self.local = send, recv, local
        self.used = 0
        self.used_local = 0
        self.col = lax.axis_index("col")
        self.row = lax.axis_index("row")
        place = lax.axis_index("dp")
        self.z = place // 2
        self.core = place % 2
        self.sibling = {"dp": self.z * 2 + (1 - self.core)}

    def peer(self, axis, step):
        if axis == "z":
            index = lax.rem(self.z + step, self.sizes["z"])
            return index, {"dp": index * 2 + self.core}
        index = lax.rem(getattr(self, axis) + step, self.sizes[axis])
        return index, {axis: index}

    def start(self, source, target, device, begin=True):
        copy = pltpu.make_async_remote_copy(
            src_ref=source,
            dst_ref=target,
            send_sem=self.send.at[self.used],
            recv_sem=self.recv.at[self.used],
            device_id=device,
            device_id_type=MESH,
        )
        self.used += 1
        if begin:
            copy.start()
        return copy

    def bring(self, source, target):
        copy = pltpu.make_async_copy(source, target, self.local.at[self.used_local])
        self.used_local += 1
        copy.start()
        return copy

    def spread(self, axis, source, target):
        return [
            self.start(source, target, self.peer(axis, step)[1])
            for step in range(1, self.sizes[axis])
        ]

    def deal(self, axis, source_of, target):
        copies = []
        for step in range(1, self.sizes[axis]):
            index, device = self.peer(axis, step)
            copies.append(self.start(source_of(index), target, device))
        return copies


def finish(copies):
    for copy in copies:
        copy.wait()


def as_rows(first, second):
    tokens = first.shape[0]
    lane = lax.broadcasted_iota(jnp.int32, (tokens, LANES), 1)
    both = jnp.where(lane == 0, first, jnp.where(lane == 1, second, 0.0))
    return both.T[:8]


def as_columns(rows):
    count, tokens = rows.shape
    return jnp.concatenate([rows, jnp.zeros((LANES - count, tokens), F32)], 0).T


def body(sizes, layers, *refs):
    (
        x_in, cot, small, qbias, ubias, wq_in, wo_in, wu_in, wd_in,
        x_out, g_out, gw, sums_out,
        wq, wo, wu, wd, smg, xg, st1, h, q, kvg, probs, og, abr, xg2, st2, h2, gp, zz, mbr,
        inv1, inv2, msend, mrecv, dmg, dur, hsend, hrecv2, bst2, osend, orecv, dob, kvsend, kvrecv,
        jg, hrecv1, bst1, grad, crecv, ra, rb, ta, tb, ua, ub, fin, fdown, sums, sumc, sumy, sumz,
        send, recv, local,
    ) = refs
    net = Links(sizes, send, recv, local)
    c, r, z, core = net.col, net.row, net.z, net.core
    ncol, nrow, nz = sizes["col"], sizes["row"], sizes["z"]
    tokens, width = x_in.shape
    hidden = ubias.shape[1]
    full = width * ncol
    length = tokens * nrow
    blocks = hidden // width
    pairs = width // LANES
    scale = HD ** (-0.5)

    barrier = pltpu.get_barrier_semaphore()
    greeted = [net.peer(a, s)[1] for a in ("col", "row", "z") for s in range(1, sizes[a])]
    greeted.append(net.sibling)
    for device in greeted:
        pl.semaphore_signal(barrier, inc=1, device_id=device, device_id_type=MESH)
    mirror = {"row": c, "col": r}

    @pl.when(r != c)
    def _():
        pl.semaphore_signal(barrier, inc=1, device_id=mirror, device_id_type=MESH)

    pl.semaphore_wait(barrier, len(greeted) + jnp.where(r != c, 1, 0))

    def flip_start(source, target):
        copy = net.start(source, target, mirror, begin=False)
        here = pltpu.make_async_copy(source, target, local.at[net.used_local])
        net.used_local += 1

        @pl.when(r != c)
        def _():
            copy.start()

        @pl.when(r == c)
        def _():
            here.start()

        return copy, here

    def flip_wait(pair):
        copy, here = pair

        @pl.when(r != c)
        def _():
            copy.wait()

        @pl.when(r == c)
        def _():
            here.wait()

    class Weight:
        def __init__(self, level, source, store, flipped=False):
            self.level, self.source, self.store, self.flipped = level, source, store, flipped

        def flip(self):
            self.turn = flip_start(self.source.at[self.level, core], self.store.at[self.level, c, core])

        def begin(self):
            place = self.store.at[self.level, r, core]
            if self.flipped:
                flip_wait(self.turn)
                self.copies = net.spread("row", place, place)
            else:
                source = self.source.at[self.level, core]
                self.copies = [net.bring(source, place)] + net.spread("row", source, place)

        def share(self):
            finish(self.copies)
            place = self.store.at[self.level, :, core]
            self.shared = net.start(place, place, net.sibling)

        def ready(self):
            self.shared.wait()

    wqs = [Weight(l, wq_in, wq) for l in range(layers)]
    wos = [Weight(l, wo_in, wo) for l in range(layers)]
    wus = [Weight(l, wu_in, wu) for l in range(layers)]
    wds = [Weight(l, wd_in, wd, True) for l in range(layers)]

    def param(level, index):
        return small[level * 9 + index : level * 9 + index + 1, :]

    def any_param(level, index, block):
        return smg[block, level * 9 + index : level * 9 + index + 1, :]

    def norm_send(value, store, stats):
        mean = jnp.sum(value, 1, keepdims=True) * (1.0 / width)
        centered = value - mean
        store[c] = centered.astype(BF)
        stats[c] = as_rows(mean, jnp.sum(centered * centered, 1, keepdims=True))
        return net.spread("col", store.at[c], store.at[c]) + net.spread("col", stats.at[c], stats.at[c])

    def norm_apply(level, first, store, stats, inverse, result):
        columns = as_columns(stats[...].reshape(ncol * 8, tokens))
        means = [columns[:, 8 * i : 8 * i + 1] for i in range(ncol)]
        mean = sum(means) * (1.0 / ncol)
        spread = sum(columns[:, 8 * i + 1 : 8 * i + 2] for i in range(ncol))
        spread = spread + width * sum((m - mean) * (m - mean) for m in means)
        scaled = lax.rsqrt(spread * (1.0 / full) + EPS)
        inverse[...] = jnp.broadcast_to(scaled, inverse.shape)
        for i in range(ncol):
            normed = (store[i].astype(F32) + (means[i] - mean)) * scaled
            store[i] = normed.astype(BF)
            result[:, i * width : (i + 1) * width] = (
                normed * any_param(level, first, i) + any_param(level, first + 1, i)
            ).astype(BF)

    def slots(store):
        return sum(store[i].astype(F32) for i in range(store.shape[0]))

    lane = lax.broadcasted_iota(jnp.int32, (tokens, LANES), 1)
    half = [(lane < HD).astype(F32), (lane >= HD).astype(F32)]

    def pick(values):
        side = lax.broadcasted_iota(jnp.int32, values[0].shape, 1)
        return jnp.where(side < HD, values[0], values[1])

    def pair_lanes(p):
        return pl.ds(pl.multiple_of(p * LANES, LANES), LANES)

    def attend(level):
        def step(p, carry):
            lanes = pair_lanes(p)
            queries = q[level, :, lanes].astype(F32)
            keys = kvg[level, :, 0, :, lanes].reshape(length, LANES)
            values = kvg[level, :, 1, :, lanes].reshape(length, LANES)
            found = []
            for side in range(2):
                scores = mm_nt((queries * half[side]).astype(BF), keys) * scale
                raised = jnp.exp(scores - jnp.max(scores, 1, keepdims=True))
                share = (raised * (1.0 / jnp.sum(raised, 1, keepdims=True))).astype(BF)
                probs[level, 2 * p + side] = share
                found.append(mm(share, values))
            og[level, c, :, lanes] = pick(found).astype(BF)
            return carry

        lax.fori_loop(0, pairs, step, 0)

    def attend_back(level):
        def step(p, carry):
            lanes = pair_lanes(p)
            queries = q[level, :, lanes]
            upstream = dob[:, lanes]
            keys = kvg[level, :, 0, :, lanes].reshape(length, LANES)
            values = kvg[level, :, 1, :, lanes].reshape(length, LANES)
            dq, dk, dv = [], [], []
            for side in range(2):
                share = probs[level, 2 * p + side]
                wide = share.astype(F32)
                pulled = mm_nt((upstream.astype(F32) * half[side]).astype(BF), values)
                inner = jnp.sum(wide * pulled, 1, keepdims=True)
                slope = (wide * (pulled - inner)).astype(BF)
                dq.append(mm(slope, keys))
                dk.append(mm_tn(slope, queries))
                dv.append(mm_tn(share, upstream))
            jg[:, lanes] = (pick(dq) * scale).astype(BF)
            kvsend[:, 0, :, lanes] = (pick(dk) * scale).astype(BF).reshape(nrow, tokens, LANES)
            kvsend[:, 1, :, lanes] = pick(dv).astype(BF).reshape(nrow, tokens, LANES)
            return carry

        lax.fori_loop(0, pairs, step, 0)

    x_out[...] = x_in[...]
    smg[c] = small[...]
    wqs[0].begin()
    first_copies = net.spread("col", smg.at[c], smg.at[c])
    for level in range(layers):
        copies = norm_send(x_out[...], xg.at[level], st1.at[level])
        if level == 0:
            finish(first_copies)
            wds[0].flip()
            wos[0].begin()
            wus[0].begin()
        finish(copies)
        norm_apply(level, 0, xg.at[level], st1.at[level], inv1.at[level], h.at[level])
        if level == 0:
            wqs[0].share()
        wqs[level].ready()

        def project(j):
            weight = wq[level, :, :, :, j * width : (j + 1) * width].reshape(full, width)
            return mm(h[level], weight)

        kvg[level, r, 0] = project(1).astype(BF)
        kvg[level, r, 1] = (project(2) + param(level, 2)).astype(BF)
        copies = net.spread("row", kvg.at[level, r], kvg.at[level, r])
        q[level] = (project(0) + qbias[level : level + 1, :]).astype(BF)
        if level == 0:
            wos[0].share()
        finish(copies)
        attend(level)
        copies = net.spread("col", og.at[level, c], og.at[level, c])
        if level == 0:
            wds[0].begin()
            wus[0].share()
        finish(copies)
        wos[level].ready()
        branch = param(level, 3)
        for i in range(ncol):
            branch = branch + mm(og[level, i], wo[level, i].reshape(width, width))
        abr[level] = branch
        middle = x_out[...] + param(level, 4) * branch
        x_out[...] = middle
        copies = norm_send(middle, xg2.at[level], st2.at[level])
        if level + 1 < layers:
            wds[level + 1].flip()
        finish(copies)
        norm_apply(level, 5, xg2.at[level], st2.at[level], inv2.at[level], h2.at[level])
        wus[level].ready()
        if level == 0:
            wds[0].share()
        if level + 1 < layers:
            wqs[level + 1].begin()

        def widen_step(j, carry):
            lanes = pl.ds(pl.multiple_of(j * width, width), width)
            pre = mm(h2[level], wu[level, :, :, :, lanes].reshape(full, width)) + ubias[level : level + 1, lanes]
            below = 0.5 * (1.0 + lax.erf(pre * (0.5**0.5)))
            zz[level, :, lanes] = (pre * below).astype(BF)
            bell = jnp.exp(-0.5 * pre * pre) * (0.5 / jnp.pi) ** 0.5
            gp[level, :, lanes] = (below + pre * bell).astype(BF)
            return carry

        lax.fori_loop(0, blocks, widen_step, 0)
        wds[level].ready()
        copies = []
        for step in range(1, ncol + 1):
            i, device = net.peer("col", step)
            part = mm(zz[level], wd[level, i].reshape(hidden, width)).astype(BF)
            if step < ncol:
                msend[i] = part
                copies.append(net.start(msend.at[i], mrecv.at[level, c], device))
            else:
                mrecv[level, c] = part
        if level + 1 < layers:
            wqs[level + 1].share()
            wos[level + 1].begin()
            wus[level + 1].begin()
            wds[level + 1].begin()
        finish(copies)
        branch = slots(mrecv.at[level]) + param(level, 7)
        mbr[level] = branch
        x_out[...] = x_out[...] + param(level, 8) * branch
        if level + 1 < layers:
            wos[level + 1].share()
            wus[level + 1].share()
            wds[level + 1].share()

    sums[...] = jnp.zeros_like(sums)
    per = 9 + 1 + blocks

    def keep(level, index, value):
        sums[level * per + index : level * per + index + 1, :] = jnp.sum(value, 0, keepdims=True)

    def norm_back_send(level, part_of, gain, normed, store, stats):
        copies, first, second = [], 0.0, 0.0
        for step in range(1, ncol + 1):
            i, device = net.peer("col", step)
            part = part_of(i)
            scaled = part * any_param(level, gain, i)
            first = first + jnp.sum(scaled, 1, keepdims=True)
            second = second + jnp.sum(scaled * normed[i].astype(F32), 1, keepdims=True)
            if step < ncol:
                hsend[i] = part.astype(BF)
                copies.append(net.start(hsend.at[i], store.at[c], device))
            else:
                store[c] = part.astype(BF)
        stats[c] = as_rows(first, second)
        return copies + net.spread("col", stats.at[c], stats.at[c])

    def norm_back(level, gain, normed_own, inverse, store, stats):
        upstream = slots(store)
        normed = normed_own.astype(F32)
        keep(level, gain, upstream * normed)
        keep(level, gain + 1, upstream)
        columns = as_columns(slots(stats))
        scaled = upstream * param(level, gain)
        shift = columns[:, 0:1] * (1.0 / full) + normed * (columns[:, 1:2] * (1.0 / full))
        return inverse[:, 0:1] * (scaled - shift)

    def put_grad(i, piece, value):
        grad[piece % 2, i, piece // 2, 0:width, :] = value.astype(BF)

    def grads_down_up(level):
        def step(i, carry):
            down = mm_tn(zz[level], dmg[level, i]).astype(BF)
            rows = hidden // (2 * nz)
            for piece in range(2 * nz):
                grad[piece % 2, i, piece // 2, width:, :] = down[piece * rows : (piece + 1) * rows]
            lanes = pl.ds(pl.multiple_of(i * width, width), width)
            up = mm_tn(h2[level, :, lanes], dur[...])
            for j in range(blocks):
                put_grad(i, 4 + j, up[:, j * width : (j + 1) * width])
            return carry

        lax.fori_loop(0, nrow, step, 0)

    def grads_out(level, low):
        def step(i, carry):
            put_grad(i, 3, mm_tn(og[level, i], low[...]))
            return carry

        lax.fori_loop(0, nrow, step, 0)

    def grads_qkv(level):
        def step(i, carry):
            lanes = pl.ds(pl.multiple_of(i * width, width), width)
            value = mm_tn(h[level, :, lanes], jg[...])
            for j in range(3):
                put_grad(i, j, value[:, j * width : (j + 1) * width])
            return carry

        lax.fori_loop(0, nrow, step, 0)

    def reduce_steps(level):
        upper = ta.shape[1]
        top, low = pl.ds(0, upper), pl.ds(upper, upper)
        copy = net.start(grad.at[1 - core], crecv, net.sibling)
        yield
        copy.wait()

        def add(i, carry):
            for j in range(nz):
                total = grad[core, i, j].astype(F32) + crecv[i, j].astype(F32)
                grad[core, i, j] = total.astype(BF)
            return carry

        lax.fori_loop(0, nrow, add, 0)
        copies = net.deal("row", lambda i: grad.at[core, i, :, top], ra.at[r])
        copies += net.deal("z", lambda i: grad.at[core, :, i, low], rb.at[z])
        yield
        finish(copies)

        def add_top(j, carry):
            total = grad[core, r, j, 0:upper].astype(F32)
            for step in range(1, nrow):
                total = total + ra[net.peer("row", step)[0], j].astype(F32)
            ta[j] = total.astype(BF)
            return carry

        def add_low(j, carry):
            total = grad[core, j, z, upper:].astype(F32)
            for step in range(1, nz):
                total = total + rb[net.peer("z", step)[0], j].astype(F32)
            tb[j] = total.astype(BF)
            return carry

        lax.fori_loop(0, nz, add_top, 0)
        lax.fori_loop(0, nrow, add_low, 0)
        copies = net.deal("z", lambda i: ta.at[i], ua.at[level, z])
        copies += net.deal("row", lambda i: tb.at[i], ub.at[level, r])
        yield
        finish(copies)
        total = ta[z].astype(F32)
        for step in range(1, nz):
            total = total + ua[level, net.peer("z", step)[0]].astype(F32)
        fin[0:upper] = total.astype(BF)
        total = tb[r].astype(F32)
        for step in range(1, nrow):
            total = total + ub[level, net.peer("row", step)[0]].astype(F32)
        fin[upper:] = total.astype(BF)
        turn = flip_start(fin.at[pl.ds(width, fin.shape[0] - width)], fdown.at[level])
        yield
        flip_wait(turn)
        gw[level, core, z, 0:width] = fin[0:width]
        gw[level, core, z, width:] = fdown[level]
        copies = net.spread("z", gw.at[level, core, z], gw.at[level, core, z])
        yield
        finish(copies)
        copy = net.start(gw.at[level, core], gw.at[level, core], net.sibling)
        yield
        copy.wait()
        yield

    g_out[...] = cot[...]
    running = None

    def advance(count=1):
        for _ in range(count):
            if running is not None:
                next(running)

    for level in reversed(range(layers)):
        last = level == 0
        upstream = g_out[...]
        keep(level, 8, upstream * mbr[level])
        scaled = upstream * param(level, 8)
        keep(level, 7, scaled)
        dmg[level, c] = scaled.astype(BF)
        copies = net.spread("col", dmg.at[level, c], dmg.at[level, c])
        advance()
        finish(copies)

        def dz_step(j, carry):
            lanes = pl.ds(pl.multiple_of(j * width, width), width)
            rows = pl.ds(pl.multiple_of((j % (blocks // 2)) * width, width), width)
            value = 0.0
            for i in range(ncol):
                weight = wd[level, i, j // (blocks // 2), rows, :]
                value = value + mm_nt(dmg[level, i], weight)
            value = value * gp[level, :, lanes].astype(F32)
            rounded = value.astype(BF)
            dur[:, lanes] = rounded
            return carry

        lax.fori_loop(0, blocks, dz_step, 0)
        for j in range(blocks):
            keep(level, 10 + j, dur[:, j * width : (j + 1) * width].astype(F32))
        copies = norm_back_send(
            level,
            lambda i: mm_nt(dur[...], wu[level, i].reshape(width, hidden)),
            5, xg2.at[level], hrecv2.at[level], bst2.at[level],
        )
        if not last:
            grads_down_up(level)
        finish(copies)
        middle = g_out[...] + norm_back(
            level, 5, xg2[level, c], inv2.at[level], hrecv2.at[level], bst2.at[level]
        )
        g_out[...] = middle
        keep(level, 4, middle * abr[level])
        scaled = middle * param(level, 4)
        keep(level, 3, scaled)
        dob[...] = scaled.astype(BF)
        copies = []
        for step in range(1, ncol + 1):
            i, device = net.peer("col", step)
            part = mm_nt(dob[...], wo[level, i].reshape(width, width)).astype(BF)
            if step < ncol:
                osend[i] = part
                copies.append(net.start(osend.at[i], orecv.at[level, c], device))
            else:
                orecv[level, c] = part
        if last:
            advance()
        grads_out(level, dob)
        finish(copies)
        dob[...] = slots(orecv.at[level]).astype(BF)
        attend_back(level)
        copies = net.deal("row", lambda i: kvsend.at[i], kvrecv.at[level, r])
        kvrecv[level, r] = kvsend[r]
        if last:
            grads_down_up(level)
        finish(copies)
        for j in range(2):
            total = sum(kvrecv[level, i, j].astype(F32) for i in range(nrow))
            jg[:, (j + 1) * width : (j + 2) * width] = total.astype(BF)
        keep(level, 9, jg[:, 0:width].astype(F32))
        keep(level, 2, jg[:, 2 * width :].astype(F32))
        copies = norm_back_send(
            level,
            lambda i: mm_nt(jg[...], wq[level, i].reshape(width, 3 * width)),
            0, xg.at[level], hrecv1.at[level], bst1.at[level],
        )
        grads_qkv(level)
        if last:
            advance(4)
        running = reduce_steps(level)
        advance()
        finish(copies)
        g_out[...] = g_out[...] + norm_back(
            level, 0, xg[level, c], inv1.at[level], hrecv1.at[level], bst1.at[level]
        )

    sharing = net.start(sums, sumc, net.sibling)
    advance()
    sharing.wait()
    sumy[r] = sums[...] + sumc[...]
    copies = net.spread("row", sumy.at[r], sumy.at[r])
    advance()
    finish(copies)
    sumz[z] = sumy[0] + sumy[1] + sumy[2] + sumy[3]
    copies = net.spread("z", sumz.at[z], sumz.at[z])
    advance()
    finish(copies)
    sums_out[...] = sumz[0] + sumz[1] + sumz[2] + sumz[3]
    advance(3)


def shards(sizes, inputs, w_qkv, w_out, w_up, w_down, small_params, query_bias, up_bias, cotangent):
    tokens, width = inputs.shape
    layers, _, hidden = w_up.shape
    ncol, nrow, nz = sizes["col"], sizes["row"], sizes["z"]
    full, half = width * ncol, width // 2
    blocks = hidden // width
    small = jnp.pad(small_params.reshape(layers * 9, width), ((0, -(layers * 9) % 8), (0, 0)))
    rows = -(-layers * (10 + blocks) // 8) * 8
    piece = width + hidden // (2 * nz)
    vmem = lambda shape, dtype=BF: pltpu.VMEM(shape, dtype)
    scratch = [
        vmem((layers, nrow, 2, half, 3 * width)),
        vmem((layers, nrow, 2, half, width)),
        vmem((layers, nrow, 2, half, hidden)),
        vmem((layers, nrow, 2, hidden // 2, width)),
        vmem((ncol,) + small.shape, F32),
        vmem((layers, ncol, tokens, width)),
        vmem((layers, ncol, 8, tokens), F32),
        vmem((layers, tokens, full)),
        vmem((layers, tokens, width)),
        vmem((layers, nrow, 2, tokens, width)),
        vmem((layers, width // HD, tokens, tokens * nrow)),
        vmem((layers, ncol, tokens, width)),
        vmem((layers, tokens, width), F32),
        vmem((layers, ncol, tokens, width)),
        vmem((layers, ncol, 8, tokens), F32),
        vmem((layers, tokens, full)),
        vmem((layers, tokens, hidden)),
        vmem((layers, tokens, hidden)),
        vmem((layers, tokens, width), F32),
        vmem((layers, tokens, LANES), F32),
        vmem((layers, tokens, LANES), F32),
        vmem((ncol, tokens, width)),
        vmem((layers, ncol, tokens, width)),
        vmem((layers, ncol, tokens, width)),
        vmem((tokens, hidden)),
        vmem((ncol, tokens, width)),
        vmem((layers, ncol, tokens, width)),
        vmem((layers, ncol, 8, tokens), F32),
        vmem((ncol, tokens, width)),
        vmem((layers, ncol, tokens, width)),
        vmem((tokens, width)),
        vmem((nrow, 2, tokens, width)),
        vmem((layers, nrow, 2, tokens, width)),
        vmem((tokens, 3 * width)),
        vmem((layers, ncol, tokens, width)),
        vmem((layers, ncol, 8, tokens), F32),
        vmem((2, nrow, nz, piece, width)),
        vmem((nrow, nz, piece, width)),
        vmem((nrow, nz, piece // 2, width)),
        vmem((nz, nrow, piece // 2, width)),
        vmem((nz, piece // 2, width)),
        vmem((nrow, piece // 2, width)),
        vmem((layers, nz, piece // 2, width)),
        vmem((layers, nrow, piece // 2, width)),
        vmem((piece, width)),
        vmem((layers, piece - width, width)),
        vmem((rows, width), F32),
        vmem((rows, width), F32),
        vmem((nrow, rows, width), F32),
        vmem((nz, rows, width), F32),
        pltpu.SemaphoreType.DMA((192,)),
        pltpu.SemaphoreType.DMA((192,)),
        pltpu.SemaphoreType.DMA((16,)),
    ]
    here = pl.BlockSpec(memory_space=pltpu.VMEM)
    far = pl.BlockSpec(memory_space=pl.ANY)
    output, input_grad, grads, sums = pl.pallas_call(
        partial(body, sizes, layers),
        out_shape=(
            jax.ShapeDtypeStruct((tokens, width), F32),
            jax.ShapeDtypeStruct((tokens, width), F32),
            jax.ShapeDtypeStruct((layers, 2, nz, piece, width), BF),
            jax.ShapeDtypeStruct((rows, width), F32),
        ),
        in_specs=[here] * 5 + [far] * 4,
        out_specs=(here,) * 4,
        scratch_shapes=scratch,
        compiler_params=pltpu.CompilerParams(
            collective_id=0, has_side_effects=True, vmem_limit_bytes=63 << 20
        ),
        name="encoder",
    )(
        inputs,
        cotangent,
        small,
        query_bias,
        up_bias,
        w_qkv.reshape(layers, 2, half, 3 * width),
        w_out.reshape(layers, 2, half, width),
        w_up.reshape(layers, 2, half, hidden),
        w_down.reshape(layers, 2, hidden // 2, width),
    )
    grads = jnp.swapaxes(grads, 1, 2).reshape(layers, 2 * nz, piece, width).astype(F32)
    sums = sums[: layers * (10 + blocks)].reshape(layers, 10 + blocks, width)
    return (
        output,
        input_grad,
        jnp.swapaxes(grads[:, 0:3, :width], 1, 2),
        grads[:, 3, :width],
        jnp.swapaxes(grads[:, 4 : 4 + blocks, :width], 1, 2).reshape(layers, width, hidden),
        grads[:, :, width:].reshape(layers, hidden, width),
        sums[:, :9],
        sums[:, 9],
        sums[:, 10:].reshape(layers, hidden),
    )


def solution(mesh):
    sizes = {"col": mesh.shape["col"], "row": mesh.shape["row"], "z": mesh.shape["dp"] // 2}
    placed = (
        P(("dp", "row"), "col"),
        P(None, "row", None, "col"),
        P(None, "row", "col"),
        P(None, "row", "col"),
        P(None, "row", "col"),
        P(None, None, "col"),
        P(None, "col"),
        P(None, "col"),
        P(("dp", "row"), "col"),
    )
    return jax.shard_map(
        partial(shards, sizes),
        mesh=mesh,
        in_specs=placed,
        out_specs=(
            P(("dp", "row"), "col"),
            P(("dp", "row"), "col"),
            P(None, "row", None, "col"),
            P(None, "row", "col"),
            P(None, "row", "col"),
            P(None, "row", "col"),
            P(None, None, "col"),
            P(None, "col"),
            P(None, "col"),
        ),
        check_vma=False,
    )
```

time: 1400 us -> 358 us (0.26)
  waiting for transfers between devices: 753 us -> 0 us
  blocking collectives: 473 us -> 0 us
  Pallas kernels: 0 us -> 335 us
  matrix products: 78.1 us -> 0 us
  other arithmetic: 30.4 us -> 2.56 us
  local copies, waits for them, and re-layouts: 41.5 us -> 18.1 us
  between operations: 16.1 us -> 0.69 us
    reduce_scatter x20 -> x0, waiting for transfers between devices: 663 us -> none  [the longest x8 155 us: narrow(): lax.psum_scatter(partial_rows.astype(jnp.bfloat16), 'col', scatter_dimens...]
    pallas_call x0 -> x1, Pallas kernels: none -> 335 us  [shards(): pl.pallas_call(partial(body, sizes, layers), out_shape=(jax.ShapeDtypeStr...]
    all_gather x20 -> x0, blocking collectives: 264 us -> none  [the longest x6 64.9 us: widen(): return lax.all_gather(part_rows, 'col', axis=1, tiled=True)]
    psum x13 -> x0, blocking collectives: 209 us -> none  [the longest x1 124 us: shards(): lax.psum((jnp.stack(small_grads), jnp.stack(query_grads), jnp.stack(bias_...]
    all_gather x8 -> x0, waiting for transfers between devices: 87.9 us -> none  [the longest x2 58 us: widen(): return lax.all_gather(part_rows, 'col', axis=1, tiled=True)]
    dot_general x36 -> x0, matrix products: 78.1 us -> none  [the longest x8 17.2 us: right_product(): lax.dot_general(upstream, weight_rows, (((1,), (1,)), ((), ())), preferre...]
    convert_element_type x14 -> x1, local copies, waits for them, and re-layouts: 17.7 us -> 0.55 us  [shards(): jnp.swapaxes(grads, 1, 2).reshape(layers, 2 * nz, piece, width).astype(F32)]
    reduce_sum x16 -> x0, other arithmetic: 15.4 us -> none  [the longest x2 3.47 us: shards(): grad_gain_two = jnp.sum(mid_norm_grad * hat_two, 0)]
  transfers between devices with their start and end apart: 28 -> 0, of which waited for: 20 -> 0; matrix products, arithmetic and copies ran while one was open for 7% -> 0% of each run, Pallas kernels for 0% -> 0%
where the time goes in v1:
time: 358 us; the launch traced here: 356 us
  Pallas kernels  335 us (94%)
  local copies, waits for them, and re-layouts  18.1 us (5%)
    pallas_call x1, Pallas kernels, shards(): pl.pallas_call(partial(body, sizes, layers), out_shape=(jax.ShapeDtypeStr...  335 us

profile of v1, /device:TPU:1, one launch (start us, length us, event | category | flops | bytes accessed | tf_op | source)
XLA Modules:
  0.0 356.0 jit_solution(12354547174200086755)
XLA Ops:
  0.6 0.7 copy.30
  1.4 0.6 pad.4.refs_2_
  2.0 1.8 copy.37
  3.8 1.7 reshape.58.refs_5_
  5.5 334.7 %encoder.1 = (f32[256,256]{1,0:T(8,128)}, f32[256,256]{1,0:T(8,128)}, bf16[2,2,4,384,256]{4,3,2,1,0:T(8,128)(2,1)}, f32[32,256]{1,0:T(8,128)}) custom-call(f32[256,256]{1,0:T(8,128)} %refs_0_.1, f32[256,256]{1,0:T(8,128)} %refs_1_.1, f32[24,256]{1,0:T(8,128)} %pad.4.refs_2_, f32[2,256]{1,0:T(2,128)} %refs_3_.1, f32[2,1024]{1,0:T(2,128)} %refs_4_.1, ...), custom_call_target="tpu_custom_call" | custom-call | tf_op jit(solution)/shard_map/encoder/pallas_call | solution.py:656
  340.1 0.8 reshape.55
  340.9 0.6 copy.42
  341.5 0.6 copy.40
  342.1 0.6 copy.36
  342.7 2.6 convert_bitcast_fusion
  345.3 0.6 copy.33
  345.9 0.8 slice_bitcast_fusion.2
  346.7 1.3 slice_bitcast_fusion.1
  348.0 1.5 slice.35
  349.6 0.2 slice_bitcast_fusion
  349.8 1.9 copy.34
  351.6 0.0 copy-start.1
  351.6 0.0 copy-start
  351.7 2.9 copy.35
  354.6 0.0 copy-done.1
  354.6 0.7 copy.45
  355.3 0.0 copy-done
  355.3 0.7 copy.46
  (3 shorter events, 0.0 us)
Async XLA Ops:
  351.6 2.9 copy-start.1
  351.6 3.6 %copy-start = (f32[256,256]{1,0:T(8,128)S(1)}, f32[256,256]{1,0:T(8,128)}, u32[]{:S(2)}) copy-start(f32[256,256]{1,0:T(8,128)} %get-tuple-element.54) | copy-start | bytes 786436

commit v2 on v1

--- a/solution.py
+++ b/solution.py
@@ -101,12 +101,12 @@
 def body(sizes, layers, *refs):
     (
         x_in, cot, small, qbias, ubias, wq_in, wo_in, wu_in, wd_in,
-        x_out, g_out, gw, sums_out,
+        x_out, g_out, gq, gout, gup, gdown, sums_out,
         wq, wo, wu, wd, smg, xg, st1, h, q, kvg, probs, og, abr, xg2, st2, h2, gp, zz, mbr,
         inv1, inv2, msend, mrecv, dmg, dur, hsend, hrecv2, bst2, osend, orecv, dob, kvsend, kvrecv,
-        jg, hrecv1, bst1, grad, crecv, ra, rb, ta, tb, ua, ub, fin, fdown, sums, sumc, sumy, sumz,
-        send, recv, local,
+        jg, hrecv1, bst1, sums, sumc, sumy, sumz, *chunk_refs, send, recv, local,
     ) = refs
+    bulk, tail = chunk_refs[: len(chunk_refs) // 2], chunk_refs[len(chunk_refs) // 2 :]
     net = Links(sizes, send, recv, local)
     c, r, z, core = net.col, net.row, net.z, net.core
     ncol, nrow, nz = sizes["col"], sizes["row"], sizes["z"]
@@ -158,20 +158,13 @@
             here.wait()
 
     class Weight:
-        def __init__(self, level, source, store, flipped=False):
-            self.level, self.source, self.store, self.flipped = level, source, store, flipped
-
-        def flip(self):
-            self.turn = flip_start(self.source.at[self.level, core], self.store.at[self.level, c, core])
+        def __init__(self, level, source, store):
+            self.level, self.source, self.store = level, source, store
 
         def begin(self):
             place = self.store.at[self.level, r, core]
-            if self.flipped:
-                flip_wait(self.turn)
-                self.copies = net.spread("row", place, place)
-            else:
-                source = self.source.at[self.level, core]
-                self.copies = [net.bring(source, place)] + net.spread("row", source, place)
+            source = self.source.at[self.level, core]
+            self.copies = [net.bring(source, place)] + net.spread("row", source, place)
 
         def share(self):
             finish(self.copies)
@@ -181,16 +174,46 @@
         def ready(self):
             self.shared.wait()
 
+    class Relayed(Weight):
+        def begin(self):
+            place = self.store.at[self.level, r, core, z]
+            self.own = net.bring(self.source.at[self.level, core], self.store.at[self.level, r, core])
+            self.copies = net.spread("row", self.source.at[self.level, core, z], place)
+
+        def relay(self):
+            finish(self.copies)
+            self.copies = [self.own]
+            for step in range(1, nrow):
+                i, _ = net.peer("row", step)
+                place = self.store.at[self.level, i, core, z]
+                self.copies += net.spread("z", place, place)
+
+    class Flipped(Weight):
+        def flip(self):
+            self.turn = flip_start(
+                self.source.at[self.level, core, z], self.store.at[self.level, c, core, z]
+            )
+
+        def begin(self):
+            place = self.store.at[self.level, r, core, z]
+            flip_wait(self.turn)
+            self.copies = net.spread("row", place, place)
+
+        def relay(self):
+            finish(self.copies)
+            place = self.store.at[self.level, :, core, z]
+            self.copies = net.spread("z", place, place)
+
     wqs = [Weight(l, wq_in, wq) for l in range(layers)]
     wos = [Weight(l, wo_in, wo) for l in range(layers)]
-    wus = [Weight(l, wu_in, wu) for l in range(layers)]
-    wds = [Weight(l, wd_in, wd, True) for l in range(layers)]
+    wus = [Relayed(l, wu_in, wu) for l in range(layers)]
+    wds = [Flipped(l, wd_in, wd) for l in range(layers)]
 
     def param(level, index):
-        return small[level * 9 + index : level * 9 + index + 1, :]
+        return small[level, index : index + 1, :]
 
     def any_param(level, index, block):
-        return smg[block, level * 9 + index : level * 9 + index + 1, :]
+        return smg[block, level, index : index + 1, :]
 
     def norm_send(value, store, stats):
         mean = jnp.sum(value, 1, keepdims=True) * (1.0 / width)
@@ -228,8 +251,9 @@
         return pl.ds(pl.multiple_of(p * LANES, LANES), LANES)
 
     def attend(level):
-        def step(p, carry):
-            lanes = pair_lanes(p)
+        copies = []
+        for p in range(pairs):
+            lanes = slice(p * LANES, (p + 1) * LANES)
             queries = q[level, :, lanes].astype(F32)
             keys = kvg[level, :, 0, :, lanes].reshape(length, LANES)
             values = kvg[level, :, 1, :, lanes].reshape(length, LANES)
@@ -240,10 +264,13 @@
                 share = (raised * (1.0 / jnp.sum(raised, 1, keepdims=True))).astype(BF)
                 probs[level, 2 * p + side] = share
                 found.append(mm(share, values))
-            og[level, c, :, lanes] = pick(found).astype(BF)
-            return carry
-
-        lax.fori_loop(0, pairs, step, 0)
+            og[level, c, p] = pick(found).astype(BF)
+            place = og.at[level, c, p]
+            copies += net.spread("col", place, place)
+        return copies
+
+    def attended(level, i):
+        return jnp.concatenate([og[level, i, p] for p in range(pairs)], 1)
 
     def attend_back(level):
         def step(p, carry):
@@ -270,20 +297,21 @@
         lax.fori_loop(0, pairs, step, 0)
 
     x_out[...] = x_in[...]
-    smg[c] = small[...]
+    smg[c, :, 0 : small.shape[1]] = small[...]
     wqs[0].begin()
     first_copies = net.spread("col", smg.at[c], smg.at[c])
     for level in range(layers):
         copies = norm_send(x_out[...], xg.at[level], st1.at[level])
         if level == 0:
-            finish(first_copies)
-            wds[0].flip()
             wos[0].begin()
             wus[0].begin()
+            wds[0].flip()
+            finish(first_copies)
         finish(copies)
         norm_apply(level, 0, xg.at[level], st1.at[level], inv1.at[level], h.at[level])
         if level == 0:
             wqs[0].share()
+            wds[0].begin()
         wqs[level].ready()
 
         def project(j):
@@ -294,36 +322,37 @@
         kvg[level, r, 1] = (project(2) + param(level, 2)).astype(BF)
         copies = net.spread("row", kvg.at[level, r], kvg.at[level, r])
         q[level] = (project(0) + qbias[level : level + 1, :]).astype(BF)
+        wus[level].relay()
+        wds[level].relay()
         if level == 0:
             wos[0].share()
         finish(copies)
-        attend(level)
-        copies = net.spread("col", og.at[level, c], og.at[level, c])
-        if level == 0:
-            wds[0].begin()
-            wus[0].share()
+        copies = attend(level)
+        wus[level].share()
+        if level + 1 < layers:
+            wqs[level + 1].begin()
+            wos[level + 1].begin()
+            wus[level + 1].begin()
+            wds[level + 1].flip()
         finish(copies)
         wos[level].ready()
         branch = param(level, 3)
         for i in range(ncol):
-            branch = branch + mm(og[level, i], wo[level, i].reshape(width, width))
+            branch = branch + mm(attended(level, i), wo[level, i].reshape(width, width))
         abr[level] = branch
         middle = x_out[...] + param(level, 4) * branch
         x_out[...] = middle
         copies = norm_send(middle, xg2.at[level], st2.at[level])
+        wds[level].share()
         if level + 1 < layers:
-            wds[level + 1].flip()
+            wds[level + 1].begin()
         finish(copies)
         norm_apply(level, 5, xg2.at[level], st2.at[level], inv2.at[level], h2.at[level])
         wus[level].ready()
-        if level == 0:
-            wds[0].share()
-        if level + 1 < layers:
-            wqs[level + 1].begin()
 
         def widen_step(j, carry):
             lanes = pl.ds(pl.multiple_of(j * width, width), width)
-            pre = mm(h2[level], wu[level, :, :, :, lanes].reshape(full, width)) + ubias[level : level + 1, lanes]
+            pre = mm(h2[level], wu[level, :, :, :, :, lanes].reshape(full, width)) + ubias[level : level + 1, lanes]
             below = 0.5 * (1.0 + lax.erf(pre * (0.5**0.5)))
             zz[level, :, lanes] = (pre * below).astype(BF)
             bell = jnp.exp(-0.5 * pre * pre) * (0.5 / jnp.pi) ** 0.5
@@ -343,17 +372,11 @@
                 mrecv[level, c] = part
         if level + 1 < layers:
             wqs[level + 1].share()
-            wos[level + 1].begin()
-            wus[level + 1].begin()
-            wds[level + 1].begin()
+            wos[level + 1].share()
         finish(copies)
         branch = slots(mrecv.at[level]) + param(level, 7)
         mbr[level] = branch
         x_out[...] = x_out[...] + param(level, 8) * branch
-        if level + 1 < layers:
-            wos[level + 1].share()
-            wus[level + 1].share()
-            wds[level + 1].share()
 
     sums[...] = jnp.zeros_like(sums)
     per = 9 + 1 + blocks
@@ -387,26 +410,28 @@
         shift = columns[:, 0:1] * (1.0 / full) + normed * (columns[:, 1:2] * (1.0 / full))
         return inverse[:, 0:1] * (scaled - shift)
 
-    def put_grad(i, piece, value):
-        grad[piece % 2, i, piece // 2, 0:width, :] = value.astype(BF)
+    pieces = 2 * nz
+    part_out, part_up = width // pieces, hidden // pieces
+
+    def put_rows(store, i, start, value):
+        rows = value.shape[0] // pieces
+        for piece in range(pieces):
+            store[piece % 2, i, piece // 2, start : start + rows, :] = value[piece * rows : (piece + 1) * rows]
 
     def grads_down_up(level):
         def step(i, carry):
-            down = mm_tn(zz[level], dmg[level, i]).astype(BF)
-            rows = hidden // (2 * nz)
-            for piece in range(2 * nz):
-                grad[piece % 2, i, piece // 2, width:, :] = down[piece * rows : (piece + 1) * rows]
+            put_rows(bulk[0], i, part_out + part_up, mm_tn(zz[level], dmg[level, i]).astype(BF))
             lanes = pl.ds(pl.multiple_of(i * width, width), width)
-            up = mm_tn(h2[level, :, lanes], dur[...])
-            for j in range(blocks):
-                put_grad(i, 4 + j, up[:, j * width : (j + 1) * width])
+            up = mm_tn(h2[level, :, lanes], dur[...]).astype(BF)
+            up = [up[:, j * width : (j + 1) * width] for j in range(blocks)]
+            put_rows(bulk[0], i, part_out, jnp.concatenate(up, 0))
             return carry
 
         lax.fori_loop(0, nrow, step, 0)
 
     def grads_out(level, low):
         def step(i, carry):
-            put_grad(i, 3, mm_tn(og[level, i], low[...]))
+            put_rows(bulk[0], i, 0, mm_tn(attended(level, i), low[...]).astype(BF))
             return carry
 
         lax.fori_loop(0, nrow, step, 0)
@@ -414,15 +439,17 @@
     def grads_qkv(level):
         def step(i, carry):
             lanes = pl.ds(pl.multiple_of(i * width, width), width)
-            value = mm_tn(h[level, :, lanes], jg[...])
+            value = mm_tn(h[level, :, lanes], jg[...]).astype(BF)
             for j in range(3):
-                put_grad(i, j, value[:, j * width : (j + 1) * width])
+                put_rows(tail[0], i, j * part_out, value[:, j * width : (j + 1) * width])
             return carry
 
         lax.fori_loop(0, nrow, step, 0)
 
-    def reduce_steps(level):
-        upper = ta.shape[1]
+    def reduce_steps(level, store, flipping):
+        grad, crecv, ra, rb, ta, tb, ua, ub, fin, flipped, land = store
+        rows = grad.shape[3]
+        upper = rows // 2
         top, low = pl.ds(0, upper), pl.ds(upper, upper)
         copy = net.start(grad.at[1 - core], crecv, net.sibling)
         yield
@@ -463,31 +490,45 @@
         total = ta[z].astype(F32)
         for step in range(1, nz):
             total = total + ua[level, net.peer("z", step)[0]].astype(F32)
-        fin[0:upper] = total.astype(BF)
+        fin[level, 0:upper] = total.astype(BF)
         total = tb[r].astype(F32)
         for step in range(1, nrow):
             total = total + ub[level, net.peer("row", step)[0]].astype(F32)
-        fin[upper:] = total.astype(BF)
-        turn = flip_start(fin.at[pl.ds(width, fin.shape[0] - width)], fdown.at[level])
+        fin[level, upper:] = total.astype(BF)
+        straight = rows - (part_up if flipping else 0)
+        if flipping:
+            turn = flip_start(fin.at[level, pl.ds(straight, part_up)], flipped.at[level])
+            yield
+            flip_wait(turn)
+            land[core, z, straight:] = flipped[level]
+        land[core, z, 0:straight] = fin[level, 0:straight]
+        copies = net.spread("z", land.at[core, z], land.at[core, z])
         yield
-        flip_wait(turn)
-        gw[level, core, z, 0:width] = fin[0:width]
-        gw[level, core, z, width:] = fdown[level]
-        copies = net.spread("z", gw.at[level, core, z], gw.at[level, core, z])
-        yield
-        finish(copies)
-        copy = net.start(gw.at[level, core], gw.at[level, core], net.sibling)
+        finish(copies)
+        copy = net.start(land.at[core], land.at[core], net.sibling)
         yield
         copy.wait()
+        for piece in range(pieces):
+            found = land[piece % 2, piece // 2]
+            some = slice(piece * part_out, (piece + 1) * part_out)
+            if flipping:
+                gout[level, some] = found[0:part_out]
+                block, inner = divmod(piece * part_up, width)
+                gup[level, inner : inner + part_up, block * width : (block + 1) * width] = found[
+                    part_out : part_out + part_up
+                ]
+                gdown[level, piece * part_up : (piece + 1) * part_up] = found[part_out + part_up :]
+            else:
+                for j in range(3):
+                    gq[level, j, some] = found[j * part_out : (j + 1) * part_out]
         yield
 
     g_out[...] = cot[...]
-    running = None
-
-    def advance(count=1):
-        for _ in range(count):
-            if running is not None:
-                next(running)
+    heavy, light = [], []
+
+    def advance(queue):
+        for steps in queue:
+            next(steps, None)
 
     for level in reversed(range(layers)):
         last = level == 0
@@ -497,19 +538,20 @@
         keep(level, 7, scaled)
         dmg[level, c] = scaled.astype(BF)
         copies = net.spread("col", dmg.at[level, c], dmg.at[level, c])
-        advance()
+        advance(heavy)
+        advance(light)
         finish(copies)
 
         def dz_step(j, carry):
             lanes = pl.ds(pl.multiple_of(j * width, width), width)
-            rows = pl.ds(pl.multiple_of((j % (blocks // 2)) * width, width), width)
+            per_half = blocks // 2
+            group = width // part_up
             value = 0.0
             for i in range(ncol):
-                weight = wd[level, i, j // (blocks // 2), rows, :]
-                value = value + mm_nt(dmg[level, i], weight)
+                weight = wd[level, i, j // per_half, pl.ds((j % per_half) * group, group)]
+                value = value + mm_nt(dmg[level, i], weight.reshape(width, width))
             value = value * gp[level, :, lanes].astype(F32)
-            rounded = value.astype(BF)
-            dur[:, lanes] = rounded
+            dur[:, lanes] = value.astype(BF)
             return carry
 
         lax.fori_loop(0, blocks, dz_step, 0)
@@ -520,8 +562,9 @@
             lambda i: mm_nt(dur[...], wu[level, i].reshape(width, hidden)),
             5, xg2.at[level], hrecv2.at[level], bst2.at[level],
         )
-        if not last:
-            grads_down_up(level)
+        advance(heavy)
+        advance(light)
+        grads_down_up(level)
         finish(copies)
         middle = g_out[...] + norm_back(
             level, 5, xg2[level, c], inv2.at[level], hrecv2.at[level], bst2.at[level]
@@ -540,16 +583,18 @@
                 copies.append(net.start(osend.at[i], orecv.at[level, c], device))
             else:
                 orecv[level, c] = part
-        if last:
-            advance()
+        advance(heavy)
+        advance(light)
         grads_out(level, dob)
+        heavy.append(reduce_steps(level, bulk, True))
+        advance(heavy[-1:])
         finish(copies)
         dob[...] = slots(orecv.at[level]).astype(BF)
         attend_back(level)
         copies = net.deal("row", lambda i: kvsend.at[i], kvrecv.at[level, r])
         kvrecv[level, r] = kvsend[r]
-        if last:
-            grads_down_up(level)
+        advance(heavy)
+        advance(light)
         finish(copies)
         for j in range(2):
             total = sum(kvrecv[level, i, j].astype(F32) for i in range(nrow))
@@ -561,29 +606,34 @@
             lambda i: mm_nt(jg[...], wq[level, i].reshape(width, 3 * width)),
             0, xg.at[level], hrecv1.at[level], bst1.at[level],
         )
+        advance(light)
         grads_qkv(level)
-        if last:
-            advance(4)
-        running = reduce_steps(level)
-        advance()
+        light.append(reduce_steps(level, tail, False))
+        advance(light[-1:])
+        advance(heavy)
         finish(copies)
         g_out[...] = g_out[...] + norm_back(
             level, 0, xg[level, c], inv1.at[level], hrecv1.at[level], bst1.at[level]
         )
 
     sharing = net.start(sums, sumc, net.sibling)
-    advance()
+    advance(light)
+    advance(heavy)
     sharing.wait()
     sumy[r] = sums[...] + sumc[...]
     copies = net.spread("row", sumy.at[r], sumy.at[r])
-    advance()
+    advance(light)
+    advance(heavy)
     finish(copies)
     sumz[z] = sumy[0] + sumy[1] + sumy[2] + sumy[3]
     copies = net.spread("z", sumz.at[z], sumz.at[z])
-    advance()
+    advance(light)
+    advance(heavy)
     finish(copies)
     sums_out[...] = sumz[0] + sumz[1] + sumz[2] + sumz[3]
-    advance(3)
+    for steps in light + heavy:
+        for _ in steps:
+            pass
 
 
 def shards(sizes, inputs, w_qkv, w_out, w_up, w_down, small_params, query_bias, up_bias, cotangent):
@@ -592,23 +642,22 @@
     ncol, nrow, nz = sizes["col"], sizes["row"], sizes["z"]
     full, half = width * ncol, width // 2
     blocks = hidden // width
-    small = jnp.pad(small_params.reshape(layers * 9, width), ((0, -(layers * 9) % 8), (0, 0)))
     rows = -(-layers * (10 + blocks) // 8) * 8
-    piece = width + hidden // (2 * nz)
+    bulk, tail = (width + 2 * hidden) // (2 * nz), 3 * width // (2 * nz)
     vmem = lambda shape, dtype=BF: pltpu.VMEM(shape, dtype)
     scratch = [
         vmem((layers, nrow, 2, half, 3 * width)),
         vmem((layers, nrow, 2, half, width)),
-        vmem((layers, nrow, 2, half, hidden)),
-        vmem((layers, nrow, 2, hidden // 2, width)),
-        vmem((ncol,) + small.shape, F32),
+        vmem((layers, nrow, 2, nz, half // nz, hidden)),
+        vmem((layers, nrow, 2, nz, hidden // (2 * nz), width)),
+        vmem((ncol, layers, 16, width), F32),
         vmem((layers, ncol, tokens, width)),
         vmem((layers, ncol, 8, tokens), F32),
         vmem((layers, tokens, full)),
         vmem((layers, tokens, width)),
         vmem((layers, nrow, 2, tokens, width)),
         vmem((layers, width // HD, tokens, tokens * nrow)),
-        vmem((layers, ncol, tokens, width)),
+        vmem((layers, ncol, width // LANES, tokens, LANES)),
         vmem((layers, tokens, width), F32),
         vmem((layers, ncol, tokens, width)),
         vmem((layers, ncol, 8, tokens), F32),
@@ -633,36 +682,45 @@
         vmem((tokens, 3 * width)),
         vmem((layers, ncol, tokens, width)),
         vmem((layers, ncol, 8, tokens), F32),
-        vmem((2, nrow, nz, piece, width)),
-        vmem((nrow, nz, piece, width)),
-        vmem((nrow, nz, piece // 2, width)),
-        vmem((nz, nrow, piece // 2, width)),
-        vmem((nz, piece // 2, width)),
-        vmem((nrow, piece // 2, width)),
-        vmem((layers, nz, piece // 2, width)),
-        vmem((layers, nrow, piece // 2, width)),
-        vmem((piece, width)),
-        vmem((layers, piece - width, width)),
         vmem((rows, width), F32),
         vmem((rows, width), F32),
         vmem((nrow, rows, width), F32),
         vmem((nz, rows, width), F32),
-        pltpu.SemaphoreType.DMA((192,)),
-        pltpu.SemaphoreType.DMA((192,)),
+    ]
+    for piece in (bulk, tail):
+        scratch += [
+            vmem((2, nrow, nz, piece, width)),
+            vmem((nrow, nz, piece, width)),
+            vmem((nrow, nz, piece // 2, width)),
+            vmem((nz, nrow, piece // 2, width)),
+            vmem((nz, piece // 2, width)),
+            vmem((nrow, piece // 2, width)),
+            vmem((layers, nz, piece // 2, width)),
+            vmem((layers, nrow, piece // 2, width)),
+            vmem((layers, piece, width)),
+            vmem((layers, hidden // (2 * nz), width)),
+            vmem((2, nz, piece, width)),
+        ]
+    scratch += [
+        pltpu.SemaphoreType.DMA((256,)),
+        pltpu.SemaphoreType.DMA((256,)),
         pltpu.SemaphoreType.DMA((16,)),
     ]
     here = pl.BlockSpec(memory_space=pltpu.VMEM)
     far = pl.BlockSpec(memory_space=pl.ANY)
-    output, input_grad, grads, sums = pl.pallas_call(
+    output, input_grad, qkv, out, up, down, sums = pl.pallas_call(
         partial(body, sizes, layers),
         out_shape=(
             jax.ShapeDtypeStruct((tokens, width), F32),
             jax.ShapeDtypeStruct((tokens, width), F32),
-            jax.ShapeDtypeStruct((layers, 2, nz, piece, width), BF),
+            jax.ShapeDtypeStruct((layers, 3, width, width), BF),
+            jax.ShapeDtypeStruct((layers, width, width), BF),
+            jax.ShapeDtypeStruct((layers, width, hidden), BF),
+            jax.ShapeDtypeStruct((layers, hidden, width), BF),
             jax.ShapeDtypeStruct((rows, width), F32),
         ),
         in_specs=[here] * 5 + [far] * 4,
-        out_specs=(here,) * 4,
+        out_specs=(here,) * 7,
         scratch_shapes=scratch,
         compiler_params=pltpu.CompilerParams(
             collective_id=0, has_side_effects=True, vmem_limit_bytes=63 << 20
@@ -671,23 +729,22 @@
     )(
         inputs,
         cotangent,
-        small,
+        small_params,
         query_bias,
         up_bias,
         w_qkv.reshape(layers, 2, half, 3 * width),
         w_out.reshape(layers, 2, half, width),
-        w_up.reshape(layers, 2, half, hidden),
-        w_down.reshape(layers, 2, hidden // 2, width),
+        w_up.reshape(layers, 2, nz, half // nz, hidden),
+        w_down.reshape(layers, 2, nz, hidden // (2 * nz), width),
     )
-    grads = jnp.swapaxes(grads, 1, 2).reshape(layers, 2 * nz, piece, width).astype(F32)
     sums = sums[: layers * (10 + blocks)].reshape(layers, 10 + blocks, width)
     return (
         output,
         input_grad,
-        jnp.swapaxes(grads[:, 0:3, :width], 1, 2),
-        grads[:, 3, :width],
-        jnp.swapaxes(grads[:, 4 : 4 + blocks, :width], 1, 2).reshape(layers, width, hidden),
-        grads[:, :, width:].reshape(layers, hidden, width),
+        jnp.swapaxes(qkv, 1, 2).astype(F32),
+        out.astype(F32),
+        up.astype(F32),
+        down.astype(F32),
         sums[:, :9],
         sums[:, 9],
         sums[:, 10:].reshape(layers, hidden),

time: 358 us -> 272 us (0.76)
  Pallas kernels: 335 us -> 256 us
  local copies, waits for them, and re-layouts: 18.1 us -> 8.2 us
  other arithmetic: 2.56 us -> 6.38 us
    pallas_call x1, Pallas kernels: 335 us -> 256 us  [shards(): pl.pallas_call(partial(body, sizes, layers), out_shape=(jax.ShapeDtypeStr...]
    convert_element_type x1 -> x4, other arithmetic: 2.56 us -> 6.38 us  [the longest x1 2.79 us: shards(): up.astype(F32)]
where the time goes in v2:
time: 272 us
  Pallas kernels  256 us (94%)
  local copies, waits for them, and re-layouts  8.2 us (3%)
  other arithmetic  6.38 us (2%)
    pallas_call x1, Pallas kernels, shards(): pl.pallas_call(partial(body, sizes, layers), out_shape=(jax.ShapeDtypeStr...  256 us

profile of v2, /device:TPU:1, one launch (start us, length us, event | category | flops | bytes accessed | tf_op | source)
XLA Modules:
  0.0 271.5 jit_solution(7188736147104836715)
XLA Ops:
  0.6 0.0 copy-start.5
  0.7 1.8 copy.26
  2.5 1.7 reshape.42.refs_5_
  4.1 0.0 copy-done.5
  4.1 0.6 copy.23.refs_2_
  4.8 256.2 %encoder.1 = (f32[256,256]{1,0:T(8,128)}, f32[256,256]{1,0:T(8,128)}, bf16[2,3,256,256]{3,2,1,0:T(8,128)(2,1)}, bf16[2,256,256]{2,1,0:T(8,128)(2,1)}, bf16[2,256...) custom-call(f32[256,256]{1,0:T(8,128)} %refs_0_.1, f32[256,256]{1,0:T(8,128)} %refs_1_.1, ...), custom_call_target="tpu_custom_call" | custom-call | tf_op jit(solution)/shard_map/encoder/pallas_call | solution.py:711
  261.0 0.0 copy-start
  261.0 0.8 reshape.40
  261.9 0.6 copy.25
  262.5 0.6 copy.29
  263.1 0.6 copy.31
  263.7 2.8 %convert_element_type.18 = f32[2,256,1024]{2,1,0:T(8,128)} convert(bf16[2,256,1024]{2,1,0:T(8,128)(2,1)} %get-tuple-element.20) | non-fusion elementwise | flops 524288 | bytes 3145728 | tf_op jit(solution)/shard_map/convert_element_type | solution.py:746
  266.5 0.0 copy-start.1
  266.5 0.0 copy-done
  266.5 0.0 copy-start.2
  266.5 1.5 convert_element_type.19
  268.0 0.0 copy-start.4
  268.0 0.0 copy-start.3
  268.0 0.0 copy-done.1
  268.0 1.3 convert_bitcast_fusion
  269.3 0.0 copy-done.2
  269.3 0.8 convert_element_type.17
  270.1 0.0 copy-done.4
  270.1 0.7 copy.34
  270.8 0.0 copy-done.3
  270.8 0.7 copy.35
  (2 shorter events, 0.0 us)
Async XLA Ops:
  0.6 3.5 %copy-start.5 = (f32[2,9,256]{2,0,1:T(2,128)S(1)}, f32[2,9,256]{2,0,1:T(2,128)}, u32[]{:S(2)}) copy-start(f32[2,9,256]{2,0,1:T(2,128)} %param.14) | copy-start | bytes 55300
  261.0 5.5 %copy-start = (bf16[2,1024,256]{2,1,0:T(8,128)(2,1)S(1)}, bf16[2,1024,256]{2,1,0:T(8,128)(2,1)}, u32[]{:S(2)}) copy-start(bf16[2,1024,256]{2,1,0:T(8,128)(2,1)} %get-tuple-element.21) | copy-start | bytes 3145732
  266.5 1.5 copy-start.1
  266.5 2.8 %copy-start.2 = (bf16[2,256,256]{2,1,0:T(8,128)(2,1)S(1)}, bf16[2,256,256]{2,1,0:T(8,128)(2,1)}, u32[]{:S(2)}) copy-start(bf16[2,256,256]{2,1,0:T(8,128)(2,1)} %get-tuple-element.19) | copy-start | bytes 786436
  268.0 2.1 copy-start.4
  268.0 2.8 %copy-start.3 = (f32[256,256]{1,0:T(8,128)S(1)}, f32[256,256]{1,0:T(8,128)}, u32[]{:S(2)}) copy-start(f32[256,256]{1,0:T(8,128)} %get-tuple-element.42) | copy-start | bytes 786436

commit v3 on v2

--- a/solution.py
+++ b/solution.py
@@ -10,6 +10,7 @@
 HD = 64
 EPS = 1e-06
 LANES = 128
+CHUNKS = 2
 BF = jnp.bfloat16
 F32 = jnp.float32
 MESH = pl.DeviceIdType.MESH
@@ -101,7 +102,7 @@
 def body(sizes, layers, *refs):
     (
         x_in, cot, small, qbias, ubias, wq_in, wo_in, wu_in, wd_in,
-        x_out, g_out, gq, gout, gup, gdown, sums_out,
+        x_out, g_out, gq, gout, gup, gdown, small_out, qbias_out, ubias_out,
         wq, wo, wu, wd, smg, xg, st1, h, q, kvg, probs, og, abr, xg2, st2, h2, gp, zz, mbr,
         inv1, inv2, msend, mrecv, dmg, dur, hsend, hrecv2, bst2, osend, orecv, dob, kvsend, kvrecv,
         jg, hrecv1, bst1, sums, sumc, sumy, sumz, *chunk_refs, send, recv, local,
@@ -117,6 +118,9 @@
     blocks = hidden // width
     pairs = width // LANES
     scale = HD ** (-0.5)
+    part = tokens // CHUNKS
+    spans = [slice(i * part, (i + 1) * part) for i in range(CHUNKS)]
+    whole = slice(0, tokens)
 
     barrier = pltpu.get_barrier_semaphore()
     greeted = [net.peer(a, s)[1] for a in ("col", "row", "z") for s in range(1, sizes[a])]
@@ -163,7 +167,10 @@
 
         def begin(self):
             place = self.store.at[self.level, r, core]
-            source = self.source.at[self.level, core]
+            if len(self.source.shape) == 5:
+                source = self.source.at[self.level, :, core]
+            else:
+                source = self.source.at[self.level, core]
             self.copies = [net.bring(source, place)] + net.spread("row", source, place)
 
         def share(self):
@@ -210,205 +217,238 @@
     wds = [Flipped(l, wd_in, wd) for l in range(layers)]
 
     def param(level, index):
-        return small[level, index : index + 1, :]
+        return small[index, level : level + 1, :]
 
     def any_param(level, index, block):
-        return smg[block, level, index : index + 1, :]
-
-    def norm_send(value, store, stats):
+        return smg[block, index, level : level + 1, :]
+
+    def norm_send(ch, value, store, stats):
         mean = jnp.sum(value, 1, keepdims=True) * (1.0 / width)
         centered = value - mean
-        store[c] = centered.astype(BF)
-        stats[c] = as_rows(mean, jnp.sum(centered * centered, 1, keepdims=True))
-        return net.spread("col", store.at[c], store.at[c]) + net.spread("col", stats.at[c], stats.at[c])
-
-    def norm_apply(level, first, store, stats, inverse, result):
-        columns = as_columns(stats[...].reshape(ncol * 8, tokens))
+        place = store.at[c, spans[ch]]
+        place[...] = centered.astype(BF)
+        stats[ch, c] = as_rows(mean, jnp.sum(centered * centered, 1, keepdims=True))
+        copies = net.spread("col", place, place)
+        return copies + net.spread("col", stats.at[ch, c], stats.at[ch, c])
+
+    def norm_apply(level, ch, first, store, stats, inverse, result):
+        columns = as_columns(stats[ch].reshape(ncol * 8, part))
         means = [columns[:, 8 * i : 8 * i + 1] for i in range(ncol)]
         mean = sum(means) * (1.0 / ncol)
         spread = sum(columns[:, 8 * i + 1 : 8 * i + 2] for i in range(ncol))
         spread = spread + width * sum((m - mean) * (m - mean) for m in means)
         scaled = lax.rsqrt(spread * (1.0 / full) + EPS)
-        inverse[...] = jnp.broadcast_to(scaled, inverse.shape)
+        inverse[spans[ch]] = jnp.broadcast_to(scaled, (part, LANES))
         for i in range(ncol):
-            normed = (store[i].astype(F32) + (means[i] - mean)) * scaled
-            store[i] = normed.astype(BF)
-            result[:, i * width : (i + 1) * width] = (
+            normed = (store[i, spans[ch]].astype(F32) + (means[i] - mean)) * scaled
+            store[i, spans[ch]] = normed.astype(BF)
+            result[spans[ch], i * width : (i + 1) * width] = (
                 normed * any_param(level, first, i) + any_param(level, first + 1, i)
             ).astype(BF)
 
-    def slots(store):
-        return sum(store[i].astype(F32) for i in range(store.shape[0]))
-
-    lane = lax.broadcasted_iota(jnp.int32, (tokens, LANES), 1)
-    half = [(lane < HD).astype(F32), (lane >= HD).astype(F32)]
+    def slots(store, rows):
+        return sum(store[i, rows].astype(F32) for i in range(store.shape[0]))
+
+    def one_head(value, side):
+        spot = lax.broadcasted_iota(jnp.int32, value.shape, 1)
+        return jnp.where((spot < HD) == (side == 0), value.astype(F32), 0.0).astype(BF)
 
     def pick(values):
         side = lax.broadcasted_iota(jnp.int32, values[0].shape, 1)
         return jnp.where(side < HD, values[0], values[1])
 
-    def pair_lanes(p):
-        return pl.ds(pl.multiple_of(p * LANES, LANES), LANES)
-
-    def attend(level):
-        copies = []
-        for p in range(pairs):
-            lanes = slice(p * LANES, (p + 1) * LANES)
-            queries = q[level, :, lanes].astype(F32)
-            keys = kvg[level, :, 0, :, lanes].reshape(length, LANES)
-            values = kvg[level, :, 1, :, lanes].reshape(length, LANES)
-            found = []
-            for side in range(2):
-                scores = mm_nt((queries * half[side]).astype(BF), keys) * scale
-                raised = jnp.exp(scores - jnp.max(scores, 1, keepdims=True))
-                share = (raised * (1.0 / jnp.sum(raised, 1, keepdims=True))).astype(BF)
-                probs[level, 2 * p + side] = share
-                found.append(mm(share, values))
-            og[level, c, p] = pick(found).astype(BF)
-            place = og.at[level, c, p]
-            copies += net.spread("col", place, place)
-        return copies
-
-    def attended(level, i):
-        return jnp.concatenate([og[level, i, p] for p in range(pairs)], 1)
-
-    def attend_back(level):
-        def step(p, carry):
-            lanes = pair_lanes(p)
-            queries = q[level, :, lanes]
-            upstream = dob[:, lanes]
-            keys = kvg[level, :, 0, :, lanes].reshape(length, LANES)
-            values = kvg[level, :, 1, :, lanes].reshape(length, LANES)
-            dq, dk, dv = [], [], []
-            for side in range(2):
-                share = probs[level, 2 * p + side]
-                wide = share.astype(F32)
-                pulled = mm_nt((upstream.astype(F32) * half[side]).astype(BF), values)
-                inner = jnp.sum(wide * pulled, 1, keepdims=True)
-                slope = (wide * (pulled - inner)).astype(BF)
-                dq.append(mm(slope, keys))
-                dk.append(mm_tn(slope, queries))
-                dv.append(mm_tn(share, upstream))
-            jg[:, lanes] = (pick(dq) * scale).astype(BF)
-            kvsend[:, 0, :, lanes] = (pick(dk) * scale).astype(BF).reshape(nrow, tokens, LANES)
-            kvsend[:, 1, :, lanes] = pick(dv).astype(BF).reshape(nrow, tokens, LANES)
-            return carry
-
-        lax.fori_loop(0, pairs, step, 0)
-
-    x_out[...] = x_in[...]
-    smg[c, :, 0 : small.shape[1]] = small[...]
+    def attend(level, p, rows):
+        lanes = slice(p * LANES, (p + 1) * LANES)
+        queries = q[level, rows, lanes]
+        keys = kvg[level, :, p, 0].reshape(length, LANES)
+        values = kvg[level, :, p, 1].reshape(length, LANES)
+        found = []
+        for side in range(2):
+            scores = mm_nt(one_head(queries, side), keys) * scale
+            raised = jnp.exp(scores - jnp.max(scores, 1, keepdims=True))
+            share = (raised * (1.0 / jnp.sum(raised, 1, keepdims=True))).astype(BF)
+            probs[level, 2 * p + side, rows] = share
+            found.append(mm(share, values))
+        place = og.at[level, c, p, rows]
+        place[...] = pick(found).astype(BF)
+        return net.spread("col", place, place)
+
+    def attended(level, i, rows):
+        return jnp.concatenate([og[level, i, p, rows] for p in range(pairs)], 1)
+
+    def attend_back(level, p):
+        lanes = slice(p * LANES, (p + 1) * LANES)
+        queries = q[level, :, lanes]
+        upstream = dob[:, lanes]
+        keys = kvg[level, :, p, 0].reshape(length, LANES)
+        values = kvg[level, :, p, 1].reshape(length, LANES)
+        dq, dk, dv = [], [], []
+        for side in range(2):
+            share = probs[level, 2 * p + side]
+            wide = share.astype(F32)
+            pulled = mm_nt(one_head(upstream, side), values)
+            inner = jnp.sum(wide * pulled, 1, keepdims=True)
+            slope = (wide * (pulled - inner)).astype(BF)
+            dq.append(mm(slope, keys))
+            dk.append(mm_tn(slope, queries))
+            dv.append(mm_tn(share, upstream))
+        jg[:, lanes] = (pick(dq) * scale).astype(BF)
+        kvsend[p, :, 0] = (pick(dk) * scale).astype(BF).reshape(nrow, tokens, LANES)
+        kvsend[p, :, 1] = pick(dv).astype(BF).reshape(nrow, tokens, LANES)
+        for j in range(2):
+            kvrecv[level, p, r, j] = kvsend[p, r, j]
+
+    smg[c, :, 0:layers] = small[...]
     wqs[0].begin()
-    first_copies = net.spread("col", smg.at[c], smg.at[c])
+    ahead = net.spread("col", smg.at[c], smg.at[c])
+    arriving = []
+    for ch in range(CHUNKS):
+        value = x_in[spans[ch]]
+        x_out[spans[ch]] = value
+        arriving.append(norm_send(ch, value, xg.at[0], st1.at[0]))
     for level in range(layers):
-        copies = norm_send(x_out[...], xg.at[level], st1.at[level])
+        more = level + 1 < layers
         if level == 0:
             wos[0].begin()
             wus[0].begin()
             wds[0].flip()
-            finish(first_copies)
-        finish(copies)
-        norm_apply(level, 0, xg.at[level], st1.at[level], inv1.at[level], h.at[level])
-        if level == 0:
-            wqs[0].share()
-            wds[0].begin()
-        wqs[level].ready()
-
-        def project(j):
-            weight = wq[level, :, :, :, j * width : (j + 1) * width].reshape(full, width)
-            return mm(h[level], weight)
-
-        kvg[level, r, 0] = project(1).astype(BF)
-        kvg[level, r, 1] = (project(2) + param(level, 2)).astype(BF)
-        copies = net.spread("row", kvg.at[level, r], kvg.at[level, r])
-        q[level] = (project(0) + qbias[level : level + 1, :]).astype(BF)
+            finish(ahead)
+        travelling = []
+        for ch in range(CHUNKS):
+            finish(arriving[ch])
+            rows = spans[ch]
+            norm_apply(level, ch, 0, xg.at[level], st1.at[level], inv1.at[level], h.at[level])
+            if ch == 0:
+                if level == 0:
+                    wqs[0].share()
+                    wds[0].begin()
+                wqs[level].ready()
+
+            def project(j):
+                return mm(h[level, rows], wq[level, :, :, j].reshape(full, width))
+
+            keys = project(1).astype(BF)
+            values = (project(2) + param(level, 2)).astype(BF)
+            for p in range(pairs):
+                lanes = slice(p * LANES, (p + 1) * LANES)
+                kvg[level, r, p, 0, rows] = keys[:, lanes]
+                kvg[level, r, p, 1, rows] = values[:, lanes]
+                place = kvg.at[level, r, p, :, rows]
+                travelling.append(net.spread("row", place, place))
+            q[level, rows] = (project(0) + qbias[level : level + 1, :]).astype(BF)
         wus[level].relay()
         wds[level].relay()
         if level == 0:
             wos[0].share()
-        finish(copies)
-        copies = attend(level)
+        for ch in range(CHUNKS):
+            finish(travelling[ch * pairs])
+        early = [attend(level, 0, whole)]
+        for p in range(1, pairs):
+            for ch in range(CHUNKS):
+                finish(travelling[ch * pairs + p])
+        late = [[attend(level, p, spans[ch]) for p in range(1, pairs)] for ch in range(CHUNKS)]
         wus[level].share()
-        if level + 1 < layers:
+        if more:
             wqs[level + 1].begin()
             wos[level + 1].begin()
             wus[level + 1].begin()
             wds[level + 1].flip()
-        finish(copies)
-        wos[level].ready()
-        branch = param(level, 3)
-        for i in range(ncol):
-            branch = branch + mm(attended(level, i), wo[level, i].reshape(width, width))
-        abr[level] = branch
-        middle = x_out[...] + param(level, 4) * branch
-        x_out[...] = middle
-        copies = norm_send(middle, xg2.at[level], st2.at[level])
+        finish(early[0])
+        arriving = []
+        for ch in range(CHUNKS):
+            rows = spans[ch]
+            for copies in late[ch]:
+                finish(copies)
+            if ch == 0:
+                wos[level].ready()
+            branch = param(level, 3)
+            for i in range(ncol):
+                branch = branch + mm(attended(level, i, rows), wo[level, i].reshape(width, width))
+            abr[level, rows] = branch
+            middle = x_out[rows] + param(level, 4) * branch
+            x_out[rows] = middle
+            arriving.append(norm_send(ch, middle, xg2.at[level], st2.at[level]))
         wds[level].share()
-        if level + 1 < layers:
+        if more:
             wds[level + 1].begin()
-        finish(copies)
-        norm_apply(level, 5, xg2.at[level], st2.at[level], inv2.at[level], h2.at[level])
-        wus[level].ready()
-
-        def widen_step(j, carry):
-            lanes = pl.ds(pl.multiple_of(j * width, width), width)
-            pre = mm(h2[level], wu[level, :, :, :, :, lanes].reshape(full, width)) + ubias[level : level + 1, lanes]
-            below = 0.5 * (1.0 + lax.erf(pre * (0.5**0.5)))
-            zz[level, :, lanes] = (pre * below).astype(BF)
-            bell = jnp.exp(-0.5 * pre * pre) * (0.5 / jnp.pi) ** 0.5
-            gp[level, :, lanes] = (below + pre * bell).astype(BF)
-            return carry
-
-        lax.fori_loop(0, blocks, widen_step, 0)
-        wds[level].ready()
-        copies = []
-        for step in range(1, ncol + 1):
-            i, device = net.peer("col", step)
-            part = mm(zz[level], wd[level, i].reshape(hidden, width)).astype(BF)
-            if step < ncol:
-                msend[i] = part
-                copies.append(net.start(msend.at[i], mrecv.at[level, c], device))
-            else:
-                mrecv[level, c] = part
-        if level + 1 < layers:
+        travelling = []
+        for ch in range(CHUNKS):
+            rows = spans[ch]
+            finish(arriving[ch])
+            norm_apply(level, ch, 5, xg2.at[level], st2.at[level], inv2.at[level], h2.at[level])
+            if ch == 0:
+                wus[level].ready()
+
+            def widen_step(j, carry):
+                lanes = pl.ds(pl.multiple_of(j * width, width), width)
+                pre = mm(h2[level, rows], wu[level, :, :, :, :, lanes].reshape(full, width))
+                pre = pre + ubias[level : level + 1, lanes]
+                below = 0.5 * (1.0 + lax.erf(pre * (0.5**0.5)))
+                zz[level, rows, lanes] = (pre * below).astype(BF)
+                bell = jnp.exp(-0.5 * pre * pre) * (0.5 / jnp.pi) ** 0.5
+                gp[level, rows, lanes] = (below + pre * bell).astype(BF)
+                return carry
+
+            lax.fori_loop(0, blocks, widen_step, 0)
+            if ch == 0:
+                wds[level].ready()
+            copies = []
+            for step in range(1, ncol + 1):
+                i, device = net.peer("col", step)
+                piece = mm(zz[level, rows], wd[level, i].reshape(hidden, width)).astype(BF)
+                if step < ncol:
+                    msend[i, rows] = piece
+                    copies.append(net.start(msend.at[i, rows], mrecv.at[level, c, rows], device))
+                else:
+                    mrecv[level, c, rows] = piece
+            travelling.append(copies)
+        if more:
             wqs[level + 1].share()
             wos[level + 1].share()
-        finish(copies)
-        branch = slots(mrecv.at[level]) + param(level, 7)
-        mbr[level] = branch
-        x_out[...] = x_out[...] + param(level, 8) * branch
+        arriving = []
+        for ch in range(CHUNKS):
+            rows = spans[ch]
+            finish(travelling[ch])
+            branch = slots(mrecv.at[level], rows) + param(level, 7)
+            mbr[level, rows] = branch
+            value = x_out[rows] + param(level, 8) * branch
+            x_out[rows] = value
+            if more:
+                arriving.append(norm_send(ch, value, xg.at[level + 1], st1.at[level + 1]))
 
     sums[...] = jnp.zeros_like(sums)
     per = 9 + 1 + blocks
 
     def keep(level, index, value):
-        sums[level * per + index : level * per + index + 1, :] = jnp.sum(value, 0, keepdims=True)
-
-    def norm_back_send(level, part_of, gain, normed, store, stats):
+        sums[level * per + index : level * per + index + 1, :] += jnp.sum(value, 0, keepdims=True)
+
+    def norm_back_send(level, ch, part_of, gain, normed, store, stats):
+        rows = spans[ch]
         copies, first, second = [], 0.0, 0.0
         for step in range(1, ncol + 1):
             i, device = net.peer("col", step)
-            part = part_of(i)
-            scaled = part * any_param(level, gain, i)
+            value = part_of(i)
+            scaled = value * any_param(level, gain, i)
             first = first + jnp.sum(scaled, 1, keepdims=True)
-            second = second + jnp.sum(scaled * normed[i].astype(F32), 1, keepdims=True)
+            second = second + jnp.sum(scaled * normed[i, rows].astype(F32), 1, keepdims=True)
             if step < ncol:
-                hsend[i] = part.astype(BF)
-                copies.append(net.start(hsend.at[i], store.at[c], device))
+                hsend[i, rows] = value.astype(BF)
+                copies.append(net.start(hsend.at[i, rows], store.at[c, rows], device))
             else:
-                store[c] = part.astype(BF)
-        stats[c] = as_rows(first, second)
-        return copies + net.spread("col", stats.at[c], stats.at[c])
-
-    def norm_back(level, gain, normed_own, inverse, store, stats):
-        upstream = slots(store)
-        normed = normed_own.astype(F32)
+                store[c, rows] = value.astype(BF)
+        stats[ch, c] = as_rows(first, second)
+        return copies + net.spread("col", stats.at[ch, c], stats.at[ch, c])
+
+    def norm_back(level, ch, gain, normed, inverse, store, stats):
+        rows = spans[ch]
+        upstream = slots(store, rows)
+        normed = normed[c, rows].astype(F32)
         keep(level, gain, upstream * normed)
         keep(level, gain + 1, upstream)
-        columns = as_columns(slots(stats))
+        columns = as_columns(sum(stats[ch, i] for i in range(ncol)))
         scaled = upstream * param(level, gain)
         shift = columns[:, 0:1] * (1.0 / full) + normed * (columns[:, 1:2] * (1.0 / full))
-        return inverse[:, 0:1] * (scaled - shift)
+        return inverse[rows, 0:1] * (scaled - shift)
 
     pieces = 2 * nz
     part_out, part_up = width // pieces, hidden // pieces
@@ -431,7 +471,7 @@
 
     def grads_out(level, low):
         def step(i, carry):
-            put_rows(bulk[0], i, 0, mm_tn(attended(level, i), low[...]).astype(BF))
+            put_rows(bulk[0], i, 0, mm_tn(attended(level, i, whole), low[...]).astype(BF))
             return carry
 
         lax.fori_loop(0, nrow, step, 0)
@@ -523,98 +563,135 @@
                     gq[level, j, some] = found[j * part_out : (j + 1) * part_out]
         yield
 
-    g_out[...] = cot[...]
     heavy, light = [], []
 
     def advance(queue):
         for steps in queue:
             next(steps, None)
 
-    for level in reversed(range(layers)):
-        last = level == 0
-        upstream = g_out[...]
-        keep(level, 8, upstream * mbr[level])
+    def branch_back(level, ch, upstream):
+        rows = spans[ch]
+        g_out[rows] = upstream
+        if level < 0:
+            return []
+        keep(level, 8, upstream * mbr[level, rows])
         scaled = upstream * param(level, 8)
         keep(level, 7, scaled)
-        dmg[level, c] = scaled.astype(BF)
-        copies = net.spread("col", dmg.at[level, c], dmg.at[level, c])
+        place = dmg.at[level, c, rows]
+        place[...] = scaled.astype(BF)
+        return net.spread("col", place, place)
+
+    arriving = [branch_back(layers - 1, ch, cot[spans[ch]]) for ch in range(CHUNKS)]
+    for level in reversed(range(layers)):
         advance(heavy)
         advance(light)
-        finish(copies)
-
-        def dz_step(j, carry):
-            lanes = pl.ds(pl.multiple_of(j * width, width), width)
-            per_half = blocks // 2
-            group = width // part_up
-            value = 0.0
-            for i in range(ncol):
-                weight = wd[level, i, j // per_half, pl.ds((j % per_half) * group, group)]
-                value = value + mm_nt(dmg[level, i], weight.reshape(width, width))
-            value = value * gp[level, :, lanes].astype(F32)
-            dur[:, lanes] = value.astype(BF)
-            return carry
-
-        lax.fori_loop(0, blocks, dz_step, 0)
+        travelling = []
+        for ch in range(CHUNKS):
+            rows = spans[ch]
+            finish(arriving[ch])
+
+            def dz_step(j, carry):
+                lanes = pl.ds(pl.multiple_of(j * width, width), width)
+                per_half = blocks // 2
+                group = width // part_up
+                value = 0.0
+                for i in range(ncol):
+                    weight = wd[level, i, j // per_half, pl.ds((j % per_half) * group, group)]
+                    value = value + mm_nt(dmg[level, i, rows], weight.reshape(width, width))
+                value = value * gp[level, rows, lanes].astype(F32)
+                dur[rows, lanes] = value.astype(BF)
+                return carry
+
+            lax.fori_loop(0, blocks, dz_step, 0)
+            travelling.append(
+                norm_back_send(
+                    level, ch, lambda i: mm_nt(dur[rows], wu[level, i].reshape(width, hidden)),
+                    5, xg2.at[level], hrecv2.at[level], bst2.at[level],
+                )
+            )
         for j in range(blocks):
             keep(level, 10 + j, dur[:, j * width : (j + 1) * width].astype(F32))
-        copies = norm_back_send(
-            level,
-            lambda i: mm_nt(dur[...], wu[level, i].reshape(width, hidden)),
-            5, xg2.at[level], hrecv2.at[level], bst2.at[level],
-        )
         advance(heavy)
         advance(light)
         grads_down_up(level)
-        finish(copies)
-        middle = g_out[...] + norm_back(
-            level, 5, xg2[level, c], inv2.at[level], hrecv2.at[level], bst2.at[level]
-        )
-        g_out[...] = middle
-        keep(level, 4, middle * abr[level])
-        scaled = middle * param(level, 4)
-        keep(level, 3, scaled)
-        dob[...] = scaled.astype(BF)
-        copies = []
-        for step in range(1, ncol + 1):
-            i, device = net.peer("col", step)
-            part = mm_nt(dob[...], wo[level, i].reshape(width, width)).astype(BF)
-            if step < ncol:
-                osend[i] = part
-                copies.append(net.start(osend.at[i], orecv.at[level, c], device))
-            else:
-                orecv[level, c] = part
+        arriving = []
+        for ch in range(CHUNKS):
+            rows = spans[ch]
+            finish(travelling[ch])
+            middle = g_out[rows] + norm_back(
+                level, ch, 5, xg2.at[level], inv2.at[level], hrecv2.at[level], bst2.at[level]
+            )
+            g_out[rows] = middle
+            keep(level, 4, middle * abr[level, rows])
+            scaled = middle * param(level, 4)
+            keep(level, 3, scaled)
+            dob[rows] = scaled.astype(BF)
+            copies = []
+            for step in range(1, ncol + 1):
+                i, device = net.peer("col", step)
+                piece = mm_nt(dob[rows], wo[level, i].reshape(width, width)).astype(BF)
+                if step < ncol:
+                    osend[i, rows] = piece
+                    copies.append(net.start(osend.at[i, rows], orecv.at[level, c, rows], device))
+                else:
+                    orecv[level, c, rows] = piece
+            arriving.append(copies)
         advance(heavy)
         advance(light)
         grads_out(level, dob)
         heavy.append(reduce_steps(level, bulk, True))
         advance(heavy[-1:])
-        finish(copies)
-        dob[...] = slots(orecv.at[level]).astype(BF)
-        attend_back(level)
-        copies = net.deal("row", lambda i: kvsend.at[i], kvrecv.at[level, r])
-        kvrecv[level, r] = kvsend[r]
+        for ch in range(CHUNKS):
+            finish(arriving[ch])
+            dob[spans[ch]] = slots(orecv.at[level], spans[ch]).astype(BF)
+        early, late = [], [[] for _ in range(CHUNKS)]
+        for p in range(pairs):
+            attend_back(level, p)
+            if p + 1 < pairs:
+                early += net.deal("row", lambda i: kvsend.at[p, i], kvrecv.at[level, p, r])
+            else:
+                for ch in range(CHUNKS):
+                    late[ch] = net.deal(
+                        "row", lambda i: kvsend.at[p, i, :, spans[ch]], kvrecv.at[level, p, r, :, spans[ch]]
+                    )
         advance(heavy)
         advance(light)
-        finish(copies)
-        for j in range(2):
-            total = sum(kvrecv[level, i, j].astype(F32) for i in range(nrow))
-            jg[:, (j + 1) * width : (j + 2) * width] = total.astype(BF)
+        finish(early)
+        travelling = []
+        for ch in range(CHUNKS):
+            rows = spans[ch]
+            finish(late[ch])
+            for p in range(pairs):
+                for j in range(2):
+                    total = sum(kvrecv[level, p, i, j, rows].astype(F32) for i in range(nrow))
+                    start = (j + 1) * width + p * LANES
+                    jg[rows, start : start + LANES] = total.astype(BF)
+
+            def dh_part(i):
+                return sum(
+                    mm_nt(jg[rows, j * width : (j + 1) * width], wq[level, i, :, j].reshape(width, width))
+                    for j in range(3)
+                )
+
+            travelling.append(
+                norm_back_send(
+                    level, ch, dh_part, 0, xg.at[level], hrecv1.at[level], bst1.at[level]
+                )
+            )
         keep(level, 9, jg[:, 0:width].astype(F32))
         keep(level, 2, jg[:, 2 * width :].astype(F32))
-        copies = norm_back_send(
-            level,
-            lambda i: mm_nt(jg[...], wq[level, i].reshape(width, 3 * width)),
-            0, xg.at[level], hrecv1.at[level], bst1.at[level],
-        )
         advance(light)
         grads_qkv(level)
         light.append(reduce_steps(level, tail, False))
         advance(light[-1:])
         advance(heavy)
-        finish(copies)
-        g_out[...] = g_out[...] + norm_back(
-            level, 0, xg[level, c], inv1.at[level], hrecv1.at[level], bst1.at[level]
-        )
+        arriving = []
+        for ch in range(CHUNKS):
+            finish(travelling[ch])
+            upstream = g_out[spans[ch]] + norm_back(
+                level, ch, 0, xg.at[level], inv1.at[level], hrecv1.at[level], bst1.at[level]
+            )
+            arriving.append(branch_back(level - 1, ch, upstream))
 
     sharing = net.start(sums, sumc, net.sibling)
     advance(light)
@@ -630,7 +707,14 @@
     advance(light)
     advance(heavy)
     finish(copies)
-    sums_out[...] = sumz[0] + sumz[1] + sumz[2] + sumz[3]
+    total = sumz[0] + sumz[1] + sumz[2] + sumz[3]
+    for level in range(layers):
+        start = level * per
+        for i in range(9):
+            small_out[i, level : level + 1, :] = total[start + i : start + i + 1]
+        qbias_out[level : level + 1, :] = total[start + 9 : start + 10]
+        for j in range(blocks):
+            ubias_out[level : level + 1, j * width : (j + 1) * width] = total[start + 10 + j : start + 11 + j]
     for steps in light + heavy:
         for _ in steps:
             pass
@@ -646,21 +730,21 @@
     bulk, tail = (width + 2 * hidden) // (2 * nz), 3 * width // (2 * nz)
     vmem = lambda shape, dtype=BF: pltpu.VMEM(shape, dtype)
     scratch = [
-        vmem((layers, nrow, 2, half, 3 * width)),
+        vmem((layers, nrow, 2, 3, half, width)),
         vmem((layers, nrow, 2, half, width)),
         vmem((layers, nrow, 2, nz, half // nz, hidden)),
         vmem((layers, nrow, 2, nz, hidden // (2 * nz), width)),
-        vmem((ncol, layers, 16, width), F32),
+        vmem((ncol, 9, 8, width), F32),
         vmem((layers, ncol, tokens, width)),
-        vmem((layers, ncol, 8, tokens), F32),
+        vmem((layers, CHUNKS, ncol, 8, tokens // CHUNKS), F32),
         vmem((layers, tokens, full)),
         vmem((layers, tokens, width)),
-        vmem((layers, nrow, 2, tokens, width)),
+        vmem((layers, nrow, width // LANES, 2, tokens, LANES)),
         vmem((layers, width // HD, tokens, tokens * nrow)),
         vmem((layers, ncol, width // LANES, tokens, LANES)),
         vmem((layers, tokens, width), F32),
         vmem((layers, ncol, tokens, width)),
-        vmem((layers, ncol, 8, tokens), F32),
+        vmem((layers, CHUNKS, ncol, 8, tokens // CHUNKS), F32),
         vmem((layers, tokens, full)),
         vmem((layers, tokens, hidden)),
         vmem((layers, tokens, hidden)),
@@ -673,15 +757,15 @@
         vmem((tokens, hidden)),
         vmem((ncol, tokens, width)),
         vmem((layers, ncol, tokens, width)),
-        vmem((layers, ncol, 8, tokens), F32),
+        vmem((layers, CHUNKS, ncol, 8, tokens // CHUNKS), F32),
         vmem((ncol, tokens, width)),
         vmem((layers, ncol, tokens, width)),
         vmem((tokens, width)),
-        vmem((nrow, 2, tokens, width)),
-        vmem((layers, nrow, 2, tokens, width)),
+        vmem((width // LANES, nrow, 2, tokens, LANES)),
+        vmem((layers, width // LANES, nrow, 2, tokens, LANES)),
         vmem((tokens, 3 * width)),
         vmem((layers, ncol, tokens, width)),
-        vmem((layers, ncol, 8, tokens), F32),
+        vmem((layers, CHUNKS, ncol, 8, tokens // CHUNKS), F32),
         vmem((rows, width), F32),
         vmem((rows, width), F32),
         vmem((nrow, rows, width), F32),
@@ -702,13 +786,13 @@
             vmem((2, nz, piece, width)),
         ]
     scratch += [
-        pltpu.SemaphoreType.DMA((256,)),
-        pltpu.SemaphoreType.DMA((256,)),
+        pltpu.SemaphoreType.DMA((384,)),
+        pltpu.SemaphoreType.DMA((384,)),
         pltpu.SemaphoreType.DMA((16,)),
     ]
     here = pl.BlockSpec(memory_space=pltpu.VMEM)
     far = pl.BlockSpec(memory_space=pl.ANY)
-    output, input_grad, qkv, out, up, down, sums = pl.pallas_call(
+    output, input_grad, qkv, out, up, down, small, query, hidden_bias = pl.pallas_call(
         partial(body, sizes, layers),
         out_shape=(
             jax.ShapeDtypeStruct((tokens, width), F32),
@@ -717,10 +801,12 @@
             jax.ShapeDtypeStruct((layers, width, width), BF),
             jax.ShapeDtypeStruct((layers, width, hidden), BF),
             jax.ShapeDtypeStruct((layers, hidden, width), BF),
-            jax.ShapeDtypeStruct((rows, width), F32),
+            jax.ShapeDtypeStruct((9, layers, width), F32),
+            jax.ShapeDtypeStruct((layers, width), F32),
+            jax.ShapeDtypeStruct((layers, hidden), F32),
         ),
         in_specs=[here] * 5 + [far] * 4,
-        out_specs=(here,) * 7,
+        out_specs=(here,) * 9,
         scratch_shapes=scratch,
         compiler_params=pltpu.CompilerParams(
             collective_id=0, has_side_effects=True, vmem_limit_bytes=63 << 20
@@ -729,15 +815,14 @@
     )(
         inputs,
         cotangent,
-        small_params,
+        jnp.swapaxes(small_params, 0, 1),
         query_bias,
         up_bias,
-        w_qkv.reshape(layers, 2, half, 3 * width),
+        jnp.swapaxes(w_qkv, 1, 2).reshape(layers, 3, 2, half, width),
         w_out.reshape(layers, 2, half, width),
         w_up.reshape(layers, 2, nz, half // nz, hidden),
         w_down.reshape(layers, 2, nz, hidden // (2 * nz), width),
     )
-    sums = sums[: layers * (10 + blocks)].reshape(layers, 10 + blocks, width)
     return (
         output,
         input_grad,
@@ -745,9 +830,9 @@
         out.astype(F32),
         up.astype(F32),
         down.astype(F32),
-        sums[:, :9],
-        sums[:, 9],
-        sums[:, 10:].reshape(layers, hidden),
+        jnp.swapaxes(small, 0, 1),
+        query,
+        hidden_bias,
     )
 
 

time: 272 us -> 241 us (0.89)
  Pallas kernels: 256 us -> 230 us
  local copies, waits for them, and re-layouts: 8.2 us -> 3.22 us
    pallas_call x1, Pallas kernels: 256 us -> 230 us  [shards(): pl.pallas_call(partial(body, sizes, layers), out_shape=(jax.ShapeDtypeStr...]
    reshape x3 -> x0, local copies, waits for them, and re-layouts: 4.34 us -> none  [the longest x2 3.49 us: shards(): w_qkv.reshape(layers, 2, half, 3 * width)]
where the time goes in v3:
time: 241 us
  Pallas kernels  230 us (95%)
  other arithmetic  6.47 us (3%)
  local copies, waits for them, and re-layouts  3.22 us (1%)
    pallas_call x1, Pallas kernels, shards(): pl.pallas_call(partial(body, sizes, layers), out_shape=(jax.ShapeDtypeStr...  230 us

profile of v3, /device:TPU:1, one launch (start us, length us, event | category | flops | bytes accessed | tf_op | source)
XLA Modules:
  0.0 240.9 jit_solution(1365770209981309444)
XLA Ops:
  0.6 230.5 %encoder.1 = (f32[256,256]{1,0:T(8,128)}, f32[256,256]{1,0:T(8,128)}, bf16[2,3,256,256]{3,2,1,0:T(8,128)(2,1)}, bf16[2,256,256]{2,1,0:T(8,128)(2,1)}, bf16[2,256...) custom-call(f32[256,256]{1,0:T(8,128)} %refs_0_.1, ...), custom_call_target="tpu_custom_call" | custom-call | tf_op jit(solution)/shard_map/encoder/pallas_call | solution.py:795
  231.1 0.0 copy-start
  231.2 2.9 %convert_element_type.18 = f32[2,256,1024]{2,1,0:T(8,128)} convert(bf16[2,256,1024]{2,1,0:T(8,128)(2,1)} %get-tuple-element.22) | non-fusion elementwise | flops 524288 | bytes 3145728 | tf_op jit(solution)/shard_map/convert_element_type | solution.py:831
  234.0 0.0 copy-start.1
  234.0 0.0 copy-done
  234.0 0.0 copy-start.2
  234.0 1.5 convert_element_type.19
  235.5 0.0 copy-start.4
  235.5 0.0 copy-start.3
  235.5 0.0 copy-done.1
  235.5 0.0 copy-start.5
  235.5 0.0 copy-start.7
  235.5 0.0 copy-start.6
  235.6 1.3 convert_bitcast_fusion
  236.8 0.0 copy-done.2
  236.8 0.8 convert_element_type.17
  237.7 0.0 copy-done.4
  237.7 0.7 copy.23
  238.4 0.0 copy-done.3
  238.4 0.7 copy.24
  239.1 0.0 copy-done.5
  239.1 0.6 copy.25
  239.7 0.0 copy-done.7
  239.7 0.6 copy.26
  240.3 0.0 copy-done.6
  240.3 0.6 copy.27
Async XLA Ops:
  231.1 2.9 %copy-start = (bf16[2,1024,256]{2,1,0:T(8,128)(2,1)S(1)}, bf16[2,1024,256]{2,1,0:T(8,128)(2,1)}, u32[]{:S(2)}) copy-start(bf16[2,1024,256]{2,1,0:T(8,128)(2,1)} %get-tuple-element.23) | copy-start | bytes 3145732
  234.0 1.5 copy-start.1
  234.0 2.8 %copy-start.2 = (bf16[2,256,256]{2,1,0:T(8,128)(2,1)S(1)}, bf16[2,256,256]{2,1,0:T(8,128)(2,1)}, u32[]{:S(2)}) copy-start(bf16[2,256,256]{2,1,0:T(8,128)(2,1)} %get-tuple-element.21) | copy-start | bytes 786436
  235.5 2.2 copy-start.4
  235.5 2.9 %copy-start.3 = (f32[256,256]{1,0:T(8,128)S(1)}, f32[256,256]{1,0:T(8,128)}, u32[]{:S(2)}) copy-start(f32[256,256]{1,0:T(8,128)} %get-tuple-element.37) | copy-start | bytes 786436
  235.5 3.6 %copy-start.5 = (f32[9,2,256]{2,1,0:T(2,128)S(1)}, f32[9,2,256]{2,1,0:T(2,128)}, u32[]{:S(2)}) copy-start(f32[9,2,256]{2,1,0:T(2,128)} %get-tuple-element.24) | copy-start | bytes 55300
  235.5 4.2 %copy-start.7 = (f32[2,256]{1,0:T(2,128)S(1)}, f32[2,256]{1,0:T(2,128)}, u32[]{:S(2)}) copy-start(f32[2,256]{1,0:T(2,128)} %get-tuple-element.43) | copy-start | bytes 6148
  235.5 4.7 %copy-start.6 = (f32[2,1024]{1,0:T(2,128)S(1)}, f32[2,1024]{1,0:T(2,128)}, u32[]{:S(2)}) copy-start(f32[2,1024]{1,0:T(2,128)} %get-tuple-element.44) | copy-start | bytes 24580
